TPU v7x, 1024 devices: a whole 4x4x32 slice. The times are simulated.
1024 devices in a mesh: dp: 128 (over y_lo, z, core), tensor: 8 (over y_hi, x).
Axes of the slice: x: 4, y: 4 (y_hi: 2, y_lo: 2; y = y_hi * 2 + y_lo), z: 32, core: 2. Of those that a mesh axis runs over, the one named last changes fastest.
Arguments:
- teacher_down: bfloat16 [4096, 28672], P('dp', 'tensor'), may hold values from -0.125 to 0.125
- kept_blocks: int32 [16], replicated, may hold values from 0 to 223, as said below
- block_slot: int32 [16], replicated, may hold values from 0 to 15, as said below
- hidden: bfloat16 [24576, 2048], P('dp', 'tensor'), may hold values from -6 to 6
- target: bfloat16 [24576, 4096], P('dp'), may hold values from -24 to 24
Outputs:
- student_out: bfloat16 [24576, 4096], P('dp', 'tensor')
- grad_down: float32 [4096, 2048], P('dp', 'tensor')
Inputs may be any that keep to these rules, and one draw needn't show every extreme that they name: `kept_blocks`: distinct teacher blocks; no teacher shard (blocks b with one value of b // 28) holds more than 4 of them, and some shard holds exactly 4. `block_slot`: each of 0 to 15 exactly once; student block s belongs to holder s // 2; at most 2 blocks of one teacher shard go to one holder, and in every draw some holder receives 2 blocks from one teacher shard.
All inputs are finite; a program needn't handle non-finite values.
Results may differ from a plain program's by a relative error of at most 0.017.
Values may be sent and summed in bfloat16 or wider, within the bound.
No kernel may reach another device: no remote copies, remote signals or barrier semaphores. Data moves between devices by JAX's collectives and lax.ppermute only.
A program may use at most 32 MiB of HBM per device.

v0:
```python
import math

import jax
import jax.numpy as jnp
from jax import lax
from jax.sharding import PartitionSpec as P

BLK = 128
SRC_MOST = 4


def select_blocks(blocks, within, chosen, slot_count, slot_of):
    wanted = jnp.arange(slot_count, dtype=jnp.int32)
    matches = chosen[None, :] & (slot_of[None, :] == wanted[:, None])
    index_of = jnp.sum(jnp.where(matches, within[None, :], 0), axis=1)
    present = jnp.any(matches, axis=1)
    picked = jnp.take(blocks, index_of, axis=1)
    return jnp.where(present[None, :, None], picked, jnp.zeros_like(picked))


def body(teacher_down, kept_blocks, block_slot, hidden, target):
    shards = lax.axis_size("tensor")
    myself = lax.axis_index("tensor")
    rows_dev = hidden.shape[0]
    own_blocks = hidden.shape[1] // BLK
    cols_dev = teacher_down.shape[0]
    shard_blocks = teacher_down.shape[1] // BLK
    blocks = teacher_down.reshape(cols_dev, shard_blocks, BLK)
    count_kept = kept_blocks.shape[0]
    source = kept_blocks // shard_blocks
    within = kept_blocks % shard_blocks
    ordinal = jnp.arange(count_kept, dtype=jnp.int32)
    earlier = ordinal[None, :] < ordinal[:, None]
    same_source = source[None, :] == source[:, None]
    mine_sent = source == myself
    my_slots = myself * own_blocks + jnp.arange(own_blocks, dtype=jnp.int32)
    needed = block_slot[None, :] == my_slots[:, None]
    position = jnp.sum((same_source & earlier).astype(jnp.int32), axis=1)
    packed = select_blocks(blocks, within, mine_sent, SRC_MOST, position)
    arrived = lax.all_gather(packed, "tensor", axis=1, tiled=True)
    located = source * SRC_MOST + position
    index_of = jnp.sum(jnp.where(needed, located[None, :], 0), axis=1)
    student = jnp.take(arrived, index_of, axis=1).reshape(cols_dev, own_blocks * BLK)
    partials = lax.dot_general(
        hidden,
        lax.all_gather(student, "dp", axis=0, tiled=True),
        (((1,), (1,)), ((), ())),
        preferred_element_type=jnp.float32,
    )
    width_out = target.shape[1] // shards
    summed_all = lax.psum(partials.astype(jnp.bfloat16), "tensor")
    student_out = lax.dynamic_slice_in_dim(summed_all, myself * width_out, width_out, 1)
    residue = (summed_all.astype(jnp.float32) - target.astype(jnp.float32)).astype(jnp.bfloat16)
    gradient = lax.psum_scatter(
        lax.dot_general(
            residue, hidden, (((0,), (0,)), ((), ())), preferred_element_type=jnp.float32
        ),
        "dp",
        scatter_dimension=0,
        tiled=True,
    )
    factor = 1.0 / math.sqrt(rows_dev * lax.axis_size("dp"))
    return (student_out, gradient * factor)


def solution(mesh):
    placed = (P("dp", "tensor"), P(), P(), P("dp", "tensor"), P("dp", None))
    return jax.shard_map(
        body,
        mesh=mesh,
        in_specs=placed,
        out_specs=(P("dp", "tensor"), P("dp", "tensor")),
        check_vma=False,
    )
```

profile of v0, /device:TPU:1, one launch (start us, length us, event | category | flops | bytes accessed | tf_op | source)
XLA Modules:
  0.0 871.6 jit_solution(874929716938397613)
XLA Ops:
  7.2 0.0 copy-start
  7.2 0.0 all-gather.2.cloned.1.call-start
  7.2 0.7 and_select_fusion
  7.9 0.7 broadcast_compare_fusion
  8.6 0.2 convert_reduce_fusion
  8.8 0.1 select_reduce_fusion
  8.9 0.1 fusion.4
  9.1 0.8 fusion.5
  10.0 0.0 copy-done
  10.0 0.6 gather_fusion
  10.6 0.1 select_bitcast_fusion
  10.7 29.8 %all_gather.6 = bf16[32,32,128]{2,0,1:T(8,128)(2,1)S(1)} all-gather(bf16[32,4,128]{2,0,1:T(8,128)(2,1)S(1)} %select_bitcast_fusion), channel_id=1, replica_groups=mesh['dp'=128,'tensor'=8] {'tensor'}, dimensions={1}, use_global_device_ids=true | all-gather | bytes 294912 | tf_op jit(solution)/shard_map/all_gather | solution.py:40
  40.5 0.1 broadcast_bitcast_fusion
  40.6 0.6 gather_fusion.1
  41.1 0.6 bitcast_select_fusion
  41.7 0.0 all-gather.2.cloned.1.call-update
  41.8 0.0 all-reduce.2.cloned.1.call-start
  41.8 248.4 %all-gather.2.cloned.1.call-done = bf16[4096,256]{1,0:T(8,128)(2,1)} async-done(((bf16[32,256]{1,0:T(8,128)(2,1)}), bf16[4096,256]{1,0:T(8,128)(2,1)}) %all-gather.2.cloned.1.call-update) | async-done | bytes 2097168 | tf_op jit(solution)/shard_map/all_gather | solution.py:46
  290.2 0.0 copy-start.2
  290.2 3.6 fusion
  293.9 0.0 copy-start.1
  293.9 0.0 all-reduce.2.cloned.1.call-update
  293.9 0.0 reduce-scatter.2.cloned.1.call-start
  293.9 114.0 %all-reduce.2.cloned.1.call-done = bf16[192,4096]{1,0:T(8,128)(2,1)} async-done(((bf16[192,4096]{1,0:T(8,128)(2,1)}), bf16[192,4096]{1,0:T(8,128)(2,1)}) %all-reduce.2.cloned.1.call-update) | async-done | bytes 1572880 | tf_op jit(solution)/shard_map/psum | solution.py:51
  407.9 0.0 copy-done.2
  407.9 0.0 copy-done.1
  408.0 4.1 fusion.1
  412.1 0.0 reduce-scatter.2.cloned.1.call-update
  412.1 1.6 constant_dynamic-slice_fusion
  413.7 449.9 %reduce-scatter.2.cloned.1.call-done = f32[32,256]{1,0:T(8,128)} async-done(((f32[4096,256]{1,0:T(8,128)}), f32[32,256]{1,0:T(8,128)}) %reduce-scatter.2.cloned.1.call-update) | async-done | bytes 32784 | tf_op jit(solution)/shard_map/reduce_scatter | solution.py:54
  863.7 1.4 broadcast_multiply_fusion
  (9 shorter events, 0.1 us)
Async XLA Ops:
  7.2 2.8 copy-start
  7.2 283.1 %all-gather.2.cloned.1.call-start = ((), (), s32[]{:S(2)}) async-start(), calls=%async_computation.1 | async-start | bytes 2113536 | tf_op jit(solution)/shard_map/all_gather | solution.py:46
  41.8 366.2 %all-reduce.2.cloned.1.call-start = ((), (), s32[]{:S(2)}) async-start(), calls=%async_computation.2 | async-start | bytes 3145728 | tf_op jit(solution)/shard_map/psum | solution.py:51
  290.2 117.7 %copy-start.2 = (bf16[192,256]{1,0:T(8,128)(2,1)S(1)}, bf16[192,256]{1,0:T(8,128)(2,1)}, u32[]{:S(2)}) copy-start(bf16[192,256]{1,0:T(8,128)(2,1)} %param.8) | copy-start | bytes 294916
  293.9 114.1 %copy-start.1 = (bf16[192,4096]{1,0:T(8,128)(2,1)S(1)}, bf16[192,4096]{1,0:T(8,128)(2,1)}, u32[]{:S(2)}) copy-start(bf16[192,4096]{1,0:T(8,128)(2,1)} %param.9) | copy-start | bytes 4718596
  293.9 569.8 %reduce-scatter.2.cloned.1.call-start = ((), (), s32[]{:S(2)}) async-start(), calls=%async_computation.3 | async-start | bytes 4227072 | tf_op jit(solution)/shard_map/reduce_scatter | solution.py:54
Sparse Core Ops, SparseCore 0:
  41.9 248.3 all-gather.1
  294.0 113.8 all-reduce.1
  412.2 451.3 reduce-scatter.1
where the time goes:
time: 875 us; the launch traced here: 872 us
  waiting for transfers between devices  812 us (93%)
  blocking collectives  29.8 us (3%)
  between operations  13.8 us (2%)
    reduce_scatter x1, waiting for transfers between devices, body(): lax.psum_scatter(lax.dot_general(residue, hidden, (((0,), (0,)), ((), ())...  450 us
    all_gather x1, waiting for transfers between devices, body(): lax.all_gather(student, 'dp', axis=0, tiled=True)  248 us
    psum x1, waiting for transfers between devices, body(): summed_all = lax.psum(partials.astype(jnp.bfloat16), 'tensor')  114 us
    all_gather x1, blocking collectives, body(): arrived = lax.all_gather(packed, 'tensor', axis=1, tiled=True)  29.8 us
  transfers between devices with their start and end apart: 3, of which 3 were waited for; matrix products, arithmetic and copies ran while one was open for 0% of the time, Pallas kernels for 0%

commit v1 on v0

v1 whole, which is shorter than its diff:
```python
import math

import jax
import jax.numpy as jnp
import numpy as np
from jax import lax
from jax.experimental import pallas as pl
from jax.experimental.pallas import tpu as pltpu
from jax.sharding import Mesh
from jax.sharding import PartitionSpec as P

BF16 = jnp.bfloat16
F32 = jnp.float32
I32 = jnp.int32

AXES = ("ylo", "zh", "zl", "core", "yhi", "x")
SIZES = (2, 8, 4, 2, 2, 4)
TENSOR = ("yhi", "x")
PLANE = ("ylo", "yhi", "x")
PAIR = ("ylo", "core")

BLK = 128
KEPT = 16
MOST = 4
NT = 8
NH = 8
NL = 4
R = 4
SHARD = 28
TOK = 192
UNITS = 256

VMEM = pl.BlockSpec(memory_space=pltpu.VMEM)
SMEM = pl.BlockSpec(memory_space=pltpu.SMEM)
PARAMS = pltpu.CompilerParams(vmem_limit_bytes=40 * 1024 * 1024)


def iota(shape, axis):
    return lax.broadcasted_iota(I32, shape, axis)


def onehot(mask):
    return jnp.where(mask, 1.0, 0.0).astype(BF16)


def call(kernel, out, specs, *args):
    return pl.pallas_call(
        kernel,
        out_shape=out,
        in_specs=specs,
        out_specs=jax.tree.map(lambda _: VMEM, out),
        compiler_params=PARAMS,
    )(*args)


def pack_kernel(kept, me, teacher, packed):
    base = me[0] * SHARD
    count = jnp.int32(0)
    places = [jnp.int32(0)] * MOST
    for j in range(KEPT):
        within = kept[j] - base
        mine = (within >= 0) & (within < SHARD)
        for p in range(MOST):
            places[p] = jnp.where(mine & (count == p), within, places[p])
        count = count + mine.astype(I32)
    rows = NT * R
    picked = jnp.concatenate(
        [teacher[:, pl.ds(pl.multiple_of(w * BLK, BLK), BLK)] for w in places], axis=0
    )
    n = MOST * rows
    o, i = iota((n, n), 0), iota((n, n), 1)
    t, p, r = o // (MOST * R), (o // R) % MOST, o % R
    order = onehot(i == p * rows + t * R + r)
    packed[...] = jnp.dot(order, picked, preferred_element_type=F32).astype(BF16)


def compact_kernel(kept, slot, arrived, piece):
    n, m = KEPT * R, NT * MOST * R
    o, i = iota((n, m), 0), iota((n, m), 1)
    shard = [(kept[j] * 2341) >> 16 for j in range(KEPT)]
    wanted = jnp.zeros((n, m), I32)
    for j in range(KEPT):
        place = jnp.int32(0)
        for k in range(j):
            place = place + (shard[k] == shard[j]).astype(I32)
        wanted = jnp.where(o // R == slot[j], (shard[j] * MOST + place) * R, wanted)
    order = onehot(i == wanted + o % R)
    rows = jnp.dot(order, arrived[...], preferred_element_type=F32).astype(BF16)
    for h in range(NH):
        piece[h] = rows


def regroup_kernel(pieces, grouped):
    x = pieces[...].astype(F32)
    rows = jnp.concatenate(
        [
            x[h, s * R : (s + 1) * R]
            for s in range(KEPT)
            for h in range(NH)
        ],
        axis=0,
    ).astype(BF16)
    for k in range(NL):
        grouped[k] = rows


def target_kernel(me, target, chosen):
    half = target.shape[1] // 2
    n = 2 * NH * NL * R
    k, j = iota((half, n), 0), iota((half, n), 1)
    core, low, high, r = j // 128, (j // 32) % NL, (j // R) % NH, j % R
    column = (high * NL + low) * 64 + core * 32 + me[0] * R + r
    order = onehot(k == column)
    for y in range(2):
        got = jnp.dot(
            target[:, y * half : (y + 1) * half], order, preferred_element_type=F32
        ).astype(BF16)
        for c in range(2):
            chosen[2 * y + c] = got[:, c * 128 : (c + 1) * 128]


def main_kernel(core, own, other, weights, target, out, gradient, full):
    c = core[0]
    for k in range(NL):
        for s in range(KEPT):
            full[k * 32 : (k + 1) * 32, s * BLK : (s + 1) * BLK] = weights[
                k, s * 32 : (s + 1) * 32, :
            ]
    residue = []
    for y in range(2):
        for rel, hidden in ((0, own), (1, other)):
            group = 2 * y + (c if rel == 0 else 1 - c)
            total = jnp.zeros((TOK, 128), F32)
            for t in range(NT):
                total = total + lax.dot_general(
                    hidden[y * NT + t],
                    full[:, t * UNITS : (t + 1) * UNITS],
                    (((1,), (1,)), ((), ())),
                    preferred_element_type=F32,
                )
            rounded = total.astype(BF16)
            out[group] = rounded
            residue.append(
                (rounded.astype(F32) - target[group].astype(F32)).astype(BF16)
            )
    for t in range(NT):
        total = jnp.zeros((128, UNITS), F32)
        for y in range(2):
            for rel, hidden in ((0, own), (1, other)):
                total = total + lax.dot_general(
                    residue[2 * y + rel],
                    hidden[y * NT + t],
                    (((0,), (0,)), ((), ())),
                    preferred_element_type=F32,
                )
        total = total.astype(BF16)
        for k in range(NL):
            for s in range(2):
                gradient[k, (2 * t + s) * 32 : (2 * t + s + 1) * 32, :] = total[
                    k * 32 : (k + 1) * 32, s * BLK : (s + 1) * BLK
                ]


def first_sum_kernel(parts, summed):
    total = parts[0].astype(F32)
    for k in range(1, NL):
        total = total + parts[k].astype(F32)
    for h in range(NH):
        summed[h] = jnp.concatenate(
            [total[s * 32 + h * R : s * 32 + (h + 1) * R] for s in range(KEPT)], axis=0
        ).astype(BF16)


def second_sum_kernel(parts, summed):
    total = parts[0].astype(F32)
    for k in range(1, NH):
        total = total + parts[k].astype(F32)
    for u in range(NT):
        summed[u] = total[u * 8 : (u + 1) * 8]


def last_kernel(factor, parts, gradient):
    for t in range(NT):
        rows = parts[t] * factor
        for s in range(2):
            gradient[t * R : (t + 1) * R, s * BLK : (s + 1) * BLK] = rows[
                s * R : (s + 1) * R
            ]


def spread_kernel(parts, blocks):
    k, j = iota((512, 512), 0), iota((512, 512), 1)
    x, half, core, odd, low, r = (
        j // 128,
        (j // 64) % 2,
        (j // 32) % 2,
        (j // 16) % 2,
        (j // R) % NL,
        j % R,
    )
    order = onehot(k == (half * 2 + core) * 128 + low * 32 + (2 * x + odd) * R + r)
    for y in range(2):
        rows = jnp.concatenate(
            [
                parts[2 * y + c, h * 96 : (h + 1) * 96, :]
                for h in range(2)
                for c in range(2)
            ],
            axis=1,
        )
        got = jnp.dot(rows, order, preferred_element_type=F32).astype(BF16)
        for i in range(4):
            blocks[4 * y + i] = got[:, i * 128 : (i + 1) * 128]


def gather_kernel(parts, out):
    rows = jnp.concatenate([parts[t] for t in range(NT)], axis=1)
    k, j = iota((1024, 512), 0), iota((1024, 512), 1)
    z, core, t, r = j // 64, (j // 32) % 2, (j // R) % NT, j % R
    lane = t * 128 + core * 32 + z * R + r
    for half in range(2):
        order = onehot(k == lane + half * 64)
        out[half * 96 : (half + 1) * 96, :] = jnp.dot(
            rows, order, preferred_element_type=F32
        ).astype(BF16)


def exchange(x, axes):
    return lax.all_to_all(x, axes, 0, 0)


def body(teacher, kept, slot, hidden, target):
    me = lax.axis_index(TENSOR).astype(I32)[None]
    core = lax.axis_index("core").astype(I32)[None]
    shape = jax.ShapeDtypeStruct

    packed = call(pack_kernel, shape((128, 128), BF16), [SMEM, SMEM, VMEM], kept, me, teacher)
    arrived = exchange(packed.reshape(NT, 16, 128), TENSOR)

    plane = exchange(jnp.broadcast_to(hidden[None], (16,) + hidden.shape), PLANE)
    chosen = call(target_kernel, shape((4, TOK, 128), BF16), [SMEM, VMEM], me, target)
    wanted = exchange(chosen, PAIR)

    piece = call(
        compact_kernel,
        shape((NH, 64, 128), BF16),
        [SMEM, SMEM, VMEM],
        kept,
        slot,
        arrived.reshape(128, 128),
    )
    pieces = exchange(piece, "zh")
    grouped = call(regroup_kernel, shape((NL, 512, 128), BF16), [VMEM], pieces)
    weights = exchange(grouped, "zl")
    swap = [(0, 1), (1, 0)]
    other = lax.ppermute(plane, "core", swap)

    out, gradient = pl.pallas_call(
        main_kernel,
        out_shape=(shape((4, TOK, 128), BF16), shape((NL, 512, 128), BF16)),
        in_specs=[SMEM, VMEM, VMEM, VMEM, VMEM],
        out_specs=(VMEM, VMEM),
        scratch_shapes=[pltpu.VMEM((128, KEPT * BLK), BF16)],
        compiler_params=PARAMS,
    )(core, plane, other, weights, wanted)

    parts = exchange(gradient, "zl")
    summed = call(first_sum_kernel, shape((NH, 64, 128), BF16), [VMEM], parts)
    parts = exchange(summed, "zh")
    summed = call(second_sum_kernel, shape((NT, 8, 128), F32), [VMEM], parts)
    parts = exchange(summed, TENSOR)
    factor = 1.0 / math.sqrt(TOK * 128)
    grad = call(
        lambda a, b: last_kernel(factor, a, b), shape((32, UNITS), F32), [VMEM], parts
    )

    groups = exchange(out, PAIR)
    blocks = call(spread_kernel, shape((NT, 96, 128), BF16), [VMEM], groups)
    blocks = exchange(blocks, TENSOR)
    student = call(gather_kernel, shape((TOK, 512), BF16), [VMEM], blocks)
    return student, grad


def solution(mesh):
    fine = Mesh(np.asarray(mesh.devices).reshape(SIZES), AXES)
    dp = ("ylo", "zh", "zl", "core")
    placed = (P(dp, TENSOR), P(), P(), P(dp, TENSOR), P(dp, None))
    return jax.shard_map(
        body,
        mesh=fine,
        in_specs=placed,
        out_specs=(P(dp, TENSOR), P(dp, TENSOR)),
        check_vma=False,
    )
```

time: 875 us -> 218 us (0.25)
  the two profiles are of different devices: /device:TPU:1 before, /device:TPU:32 now
where the time goes in v1:
time: 218 us; the launch traced here: 217 us
  waiting for transfers between devices  87.6 us (40%)
  blocking collectives  75 us (34%)
  starting transfers between devices  37.3 us (17%)
  Pallas kernels  11.7 us (5%)
  local copies, waits for them, and re-layouts  4.32 us (2%)
    all_to_all x8, waiting for transfers between devices, exchange(): return lax.all_to_all(x, axes, 0, 0)  84.1 us
    all_to_all x2, blocking collectives, exchange(): return lax.all_to_all(x, axes, 0, 0)  75 us
    all_to_all x8, starting transfers between devices, exchange(): return lax.all_to_all(x, axes, 0, 0)  35.4 us
    pallas_call x9, Pallas kernels, call(): pl.pallas_call(kernel, out_shape=out, in_specs=specs, out_specs=jax.tree....  8.6 us
  transfers between devices with their start and end apart: 9, of which 9 were waited for; matrix products, arithmetic and copies ran while one was open for 0% of the time, Pallas kernels for 3%

profile of v1, /device:TPU:32, one launch (start us, length us, event | category | flops | bytes accessed | tf_op | source)
XLA Modules:
  0.0 216.7 jit_solution(13973563441386736943)
XLA Ops:
  0.6 0.0 copy-start.3
  0.6 0.0 copy-start.4
  0.7 0.0 copy-start.1
  0.7 0.9 copy-done.1
  1.6 0.0 copy-start.2
  1.6 0.7 copy-done.2
  2.3 0.0 copy-start.5
  2.3 1.4 shard_map.68
  3.7 6.9 %all-to-all-start.1 = ((bf16[8,16,128]{2,1,0:T(8,128)(2,1)}), bf16[8,16,128]{2,1,0:T(8,128)(2,1)S(1)}, u32[]{:S(2)}, u32[]{:S(2)}) async-start(bf16[8,16,128]{2,1,0:T(8,128)(2,1)} %bitcast.2), calls=%async_computation.1 | async-start | bytes 65536 | tf_op jit(solution)/shard_map/all_to_all | solution.py:229
  10.6 0.0 copy-start
  10.6 1.4 copy-done
  12.0 1.3 shard_map.71
  13.3 5.1 %all-to-all-done.1 = bf16[8,16,128]{2,1,0:T(8,128)(2,1)S(1)} async-done(((bf16[8,16,128]{2,1,0:T(8,128)(2,1)}), bf16[8,16,128]{2,1,0:T(8,128)(2,1)S(1)}, u32[]{:S(2)}, u32[]{:S(2)}) %all-to-all-start.1) | async-done | bytes 32800 | tf_op jit(solution)/shard_map/all_to_all | solution.py:229
  18.4 3.4 %all-to-all-start.4 = ((bf16[4,192,128]{2,1,0:T(8,128)(2,1)}), bf16[4,192,128]{2,1,0:T(8,128)(2,1)S(1)}, u32[]{:S(2)}, u32[]{:S(2)}) async-start(bf16[4,192,128]{2,1,0:T(8,128)(2,1)} %shard_map.71), calls=%async_computation.4 | async-start | bytes 393216 | tf_op jit(solution)/shard_map/all_to_all | solution.py:229
  21.8 0.0 copy-done.3
  21.8 0.0 copy-done.4
  21.8 0.8 shard_map.69
  22.6 4.4 %all-to-all-done.4.target = bf16[4,192,128]{2,1,0:T(8,128)(2,1)S(1)} async-done(((bf16[4,192,128]{2,1,0:T(8,128)(2,1)}), bf16[4,192,128]{2,1,0:T(8,128)(2,1)S(1)}, u32[]{:S(2)}, u32[]{:S(2)}) %all-to-all-start.4) | async-done | bytes 196640 | tf_op jit(solution)/shard_map/all_to_all | solution.py:229
  27.1 57.1 %all_to_all.50.pieces = bf16[8,64,128]{2,1,0:T(8,128)(2,1)S(1)} all-to-all(bf16[8,64,128]{2,1,0:T(8,128)(2,1)S(1)} %shard_map.69), channel_id=1, replica_groups=mesh['ylo'=2,'zh'=8,'zl'=4,'core'=2,'yhi'=2,'x'=4] {'zh'}, dimensions={0} | all-to-all | bytes 262144 | tf_op jit(solution)/shard_map/all_to_all | solution.py:229
  84.2 0.0 copy-done.5
  84.2 1.3 broadcast_in_dim.13
  85.5 3.7 %all-to-all-start = ((bf16[16,192,256]{2,1,0:T(8,128)(2,1)}), bf16[16,192,256]{2,1,0:T(8,128)(2,1)S(1)}, u32[]{:S(2)}, u32[]{:S(2)}) async-start(bf16[16,192,256]{2,1,0:T(8,128)(2,1)} %broadcast_in_dim.13), calls=%async_computation | async-start | bytes 3145728 | tf_op jit(solution)/shard_map/all_to_all | solution.py:229
  89.2 0.8 shard_map.70
  90.1 22.0 %all-to-all-done.own = bf16[16,192,256]{2,1,0:T(8,128)(2,1)S(1)} async-done(((bf16[16,192,256]{2,1,0:T(8,128)(2,1)}), bf16[16,192,256]{2,1,0:T(8,128)(2,1)S(1)}, u32[]{:S(2)}, u32[]{:S(2)}) %all-to-all-start) | async-done | bytes 1572896 | tf_op jit(solution)/shard_map/all_to_all | solution.py:229
  112.0 3.5 %all-to-all-start.3 = ((bf16[4,512,128]{2,1,0:T(8,128)(2,1)}), bf16[4,512,128]{2,1,0:T(8,128)(2,1)S(1)}, u32[]{:S(2)}, u32[]{:S(2)}) async-start(bf16[4,512,128]{2,1,0:T(8,128)(2,1)} %shard_map.70), calls=%async_computation.3 | async-start | bytes 1048576 | tf_op jit(solution)/shard_map/all_to_all | solution.py:229
  115.6 1.9 collective-permute-start
  117.5 3.5 %collective-permute-done.other = bf16[16,192,256]{2,1,0:T(8,128)(2,1)} collective-permute-done((bf16[16,192,256]{2,1,0:T(8,128)(2,1)S(1)}, bf16[16,192,256]{2,1,0:T(8,128)(2,1)}, u32[]{:S(2)}, u32[]{:S(2)}) %collective-permute-start) | collective-permute-done | bytes 1572896 | tf_op jit(solution)/shard_map/ppermute | solution.py:256
  121.0 4.3 %all-to-all-done.3.weights = bf16[4,512,128]{2,1,0:T(8,128)(2,1)S(1)} async-done(((bf16[4,512,128]{2,1,0:T(8,128)(2,1)}), bf16[4,512,128]{2,1,0:T(8,128)(2,1)S(1)}, u32[]{:S(2)}, u32[]{:S(2)}) %all-to-all-start.3) | async-done | bytes 524320 | tf_op jit(solution)/shard_map/all_to_all | solution.py:229
  125.3 3.1 %shard_map.72 = (bf16[4,192,128]{2,1,0:T(8,128)(2,1)}, bf16[4,512,128]{2,1,0:T(8,128)(2,1)S(1)}) custom-call(s32[1]{0:T(128)} %bitcast.core, bf16[16,192,256]{2,1,0:T(8,128)(2,1)S(1)} %all-to-all-done.own, bf16[16,192,256]{2,1,0:T(8,128)(2,1)} %collective-permute-done.other, bf16[4,512,128]{2,1,0:T(8,128)(2,1)S(1)} %all-to-all-done.3.weights, ...), custom_call_target="tpu_custom_call" | custom-call | tf_op jit(solution)/shard_map/pallas_call | solution.py:258
  128.4 17.9 %all_to_all.51.parts = bf16[4,512,128]{2,1,0:T(8,128)(2,1)S(1)} all-to-all(bf16[4,512,128]{2,1,0:T(8,128)(2,1)S(1)} %get-tuple-element.5), channel_id=1, replica_groups=mesh['ylo'=2,'zh'=8,'zl'=4,'core'=2,'yhi'=2,'x'=4] {'zl'}, dimensions={0} | all-to-all | bytes 1048576 | tf_op jit(solution)/shard_map/all_to_all | solution.py:229
  146.3 3.4 %all-to-all-start.5 = ((bf16[4,192,128]{2,1,0:T(8,128)(2,1)}), bf16[4,192,128]{2,1,0:T(8,128)(2,1)S(1)}, u32[]{:S(2)}, u32[]{:S(2)}) async-start(bf16[4,192,128]{2,1,0:T(8,128)(2,1)} %get-tuple-element.4), calls=%async_computation.5 | async-start | bytes 393216 | tf_op jit(solution)/shard_map/all_to_all | solution.py:229
  149.7 0.7 shard_map.75
  150.4 4.6 %all-to-all-done.5.parts = bf16[4,192,128]{2,1,0:T(8,128)(2,1)S(1)} async-done(((bf16[4,192,128]{2,1,0:T(8,128)(2,1)}), bf16[4,192,128]{2,1,0:T(8,128)(2,1)S(1)}, u32[]{:S(2)}, u32[]{:S(2)}) %all-to-all-start.5) | async-done | bytes 196640 | tf_op jit(solution)/shard_map/all_to_all | solution.py:229
  155.0 7.7 %all-to-all-start.8 = ((bf16[8,64,128]{2,1,0:T(8,128)(2,1)}), bf16[8,64,128]{2,1,0:T(8,128)(2,1)S(1)}, u32[]{:S(2)}, u32[]{:S(2)}) async-start(bf16[8,64,128]{2,1,0:T(8,128)(2,1)} %shard_map.75), calls=%async_computation.8 | async-start | bytes 262144 | tf_op jit(solution)/shard_map/all_to_all | solution.py:229
  162.6 1.1 shard_map.73
  163.7 29.4 %all-to-all-done.8.parts = bf16[8,64,128]{2,1,0:T(8,128)(2,1)S(1)} async-done(((bf16[8,64,128]{2,1,0:T(8,128)(2,1)}), bf16[8,64,128]{2,1,0:T(8,128)(2,1)S(1)}, u32[]{:S(2)}, u32[]{:S(2)}) %all-to-all-start.8) | async-done | bytes 131104 | tf_op jit(solution)/shard_map/all_to_all | solution.py:229
  193.0 3.5 %all-to-all-start.6 = ((bf16[8,96,128]{2,1,0:T(8,128)(2,1)}), bf16[8,96,128]{2,1,0:T(8,128)(2,1)S(1)}, u32[]{:S(2)}, u32[]{:S(2)}) async-start(bf16[8,96,128]{2,1,0:T(8,128)(2,1)} %shard_map.73), calls=%async_computation.6 | async-start | bytes 393216 | tf_op jit(solution)/shard_map/all_to_all | solution.py:229
  196.6 0.6 shard_map.76
  197.2 7.8 %all-to-all-done.6.parts = bf16[8,96,128]{2,1,0:T(8,128)(2,1)S(1)} async-done(((bf16[8,96,128]{2,1,0:T(8,128)(2,1)}), bf16[8,96,128]{2,1,0:T(8,128)(2,1)S(1)}, u32[]{:S(2)}, u32[]{:S(2)}) %all-to-all-start.6) | async-done | bytes 196640 | tf_op jit(solution)/shard_map/all_to_all | solution.py:229
  205.0 3.3 %all-to-all-start.9 = ((f32[8,8,128]{2,1,0:T(8,128)}), f32[8,8,128]{2,1,0:T(8,128)S(1)}, u32[]{:S(2)}, u32[]{:S(2)}) async-start(f32[8,8,128]{2,1,0:T(8,128)} %shard_map.76), calls=%async_computation.9 | async-start | bytes 65536 | tf_op jit(solution)/shard_map/all_to_all | solution.py:229
  208.4 1.2 shard_map.74
  209.5 6.5 %all-to-all-done.9.a = f32[8,8,128]{2,1,0:T(8,128)S(1)} async-done(((f32[8,8,128]{2,1,0:T(8,128)}), f32[8,8,128]{2,1,0:T(8,128)S(1)}, u32[]{:S(2)}, u32[]{:S(2)}) %all-to-all-start.9) | async-done | bytes 32800 | tf_op jit(solution)/shard_map/all_to_all | solution.py:229
  216.1 0.6 shard_map.77
Async XLA Ops:
  0.6 21.1 %copy-start.3 = (s32[16]{0:T(128)S(1)}, s32[16]{0:T(128)}, u32[]{:S(2)}) copy-start(s32[16]{0:T(128)} %kept.3) | copy-start | bytes 196
  0.6 21.1 %copy-start.4 = (s32[16]{0:T(128)S(1)}, s32[16]{0:T(128)}, u32[]{:S(2)}) copy-start(s32[16]{0:T(128)} %slot.1) | copy-start | bytes 196
  0.7 0.9 copy-start.1
  1.6 0.7 copy-start.2
  2.3 81.9 %copy-start.5 = (bf16[192,256]{1,0:T(8,128)(2,1)S(1)}, bf16[192,256]{1,0:T(8,128)(2,1)}, u32[]{:S(2)}) copy-start(bf16[192,256]{1,0:T(8,128)(2,1)} %param.8) | copy-start | bytes 294916
  3.7 14.7 %all-to-all-start.1 = ((bf16[8,16,128]{2,1,0:T(8,128)(2,1)}), bf16[8,16,128]{2,1,0:T(8,128)(2,1)S(1)}, u32[]{:S(2)}, u32[]{:S(2)}) async-start(bf16[8,16,128]{2,1,0:T(8,128)(2,1)} %bitcast.2), calls=%async_computation.1 | async-start | bytes 65536 | tf_op jit(solution)/shard_map/all_to_all | solution.py:229
  10.6 1.4 copy-start
  18.4 8.7 %all-to-all-start.4 = ((bf16[4,192,128]{2,1,0:T(8,128)(2,1)}), bf16[4,192,128]{2,1,0:T(8,128)(2,1)S(1)}, u32[]{:S(2)}, u32[]{:S(2)}) async-start(bf16[4,192,128]{2,1,0:T(8,128)(2,1)} %shard_map.71), calls=%async_computation.4 | async-start | bytes 393216 | tf_op jit(solution)/shard_map/all_to_all | solution.py:229
  85.5 26.5 %all-to-all-start = ((bf16[16,192,256]{2,1,0:T(8,128)(2,1)}), bf16[16,192,256]{2,1,0:T(8,128)(2,1)S(1)}, u32[]{:S(2)}, u32[]{:S(2)}) async-start(bf16[16,192,256]{2,1,0:T(8,128)(2,1)} %broadcast_in_dim.13), calls=%async_computation | async-start | bytes 3145728 | tf_op jit(solution)/shard_map/all_to_all | solution.py:229
  112.0 13.3 %all-to-all-start.3 = ((bf16[4,512,128]{2,1,0:T(8,128)(2,1)}), bf16[4,512,128]{2,1,0:T(8,128)(2,1)S(1)}, u32[]{:S(2)}, u32[]{:S(2)}) async-start(bf16[4,512,128]{2,1,0:T(8,128)(2,1)} %shard_map.70), calls=%async_computation.3 | async-start | bytes 1048576 | tf_op jit(solution)/shard_map/all_to_all | solution.py:229
  115.6 5.4 %collective-permute-start = (bf16[16,192,256]{2,1,0:T(8,128)(2,1)S(1)}, bf16[16,192,256]{2,1,0:T(8,128)(2,1)}, u32[]{:S(2)}, u32[]{:S(2)}) collective-permute-start(bf16[16,192,256]{2,1,0:T(8,128)(2,1)S(1)} %all-to-all-done.own), channel_id=1, source_target_pairs={{0,8},{8,0},{1,9},{9,1},{2,10},{10,2},{3,11},{11,3},{4,12},{12,4},... | collective-permute-start | bytes 4718600 | tf_op jit(solution)/shard_map/ppermute | solution.py:256
  146.3 8.7 %all-to-all-start.5 = ((bf16[4,192,128]{2,1,0:T(8,128)(2,1)}), bf16[4,192,128]{2,1,0:T(8,128)(2,1)S(1)}, u32[]{:S(2)}, u32[]{:S(2)}) async-start(bf16[4,192,128]{2,1,0:T(8,128)(2,1)} %get-tuple-element.4), calls=%async_computation.5 | async-start | bytes 393216 | tf_op jit(solution)/shard_map/all_to_all | solution.py:229
  155.0 38.1 %all-to-all-start.8 = ((bf16[8,64,128]{2,1,0:T(8,128)(2,1)}), bf16[8,64,128]{2,1,0:T(8,128)(2,1)S(1)}, u32[]{:S(2)}, u32[]{:S(2)}) async-start(bf16[8,64,128]{2,1,0:T(8,128)(2,1)} %shard_map.75), calls=%async_computation.8 | async-start | bytes 262144 | tf_op jit(solution)/shard_map/all_to_all | solution.py:229
  193.0 12.0 %all-to-all-start.6 = ((bf16[8,96,128]{2,1,0:T(8,128)(2,1)}), bf16[8,96,128]{2,1,0:T(8,128)(2,1)S(1)}, u32[]{:S(2)}, u32[]{:S(2)}) async-start(bf16[8,96,128]{2,1,0:T(8,128)(2,1)} %shard_map.73), calls=%async_computation.6 | async-start | bytes 393216 | tf_op jit(solution)/shard_map/all_to_all | solution.py:229
  205.0 11.0 %all-to-all-start.9 = ((f32[8,8,128]{2,1,0:T(8,128)}), f32[8,8,128]{2,1,0:T(8,128)S(1)}, u32[]{:S(2)}, u32[]{:S(2)}) async-start(f32[8,8,128]{2,1,0:T(8,128)} %shard_map.76), calls=%async_computation.9 | async-start | bytes 65536 | tf_op jit(solution)/shard_map/all_to_all | solution.py:229

commit v2 on v1

v2 whole, which is shorter than its diff:
```python
import math

import jax
import jax.numpy as jnp
import numpy as np
from jax import lax
from jax.experimental import pallas as pl
from jax.experimental.pallas import tpu as pltpu
from jax.sharding import Mesh
from jax.sharding import PartitionSpec as P

BF16 = jnp.bfloat16
F32 = jnp.float32
I32 = jnp.int32

AXES = ("ylo", "zh", "zl", "core", "yhi", "x")
SIZES = (2, 8, 4, 2, 2, 4)
TENSOR = ("yhi", "x")
PLANE = ("ylo", "yhi", "x")
PAIR = ("ylo", "core")

BLK = 128
KEPT = 16
MOST = 4
NT = 8
NH = 8
NL = 4
R = 4
SHARD = 28
TOK = 192
UNITS = 256

VMEM = pl.BlockSpec(memory_space=pltpu.VMEM)
SMEM = pl.BlockSpec(memory_space=pltpu.SMEM)
PARAMS = pltpu.CompilerParams(vmem_limit_bytes=40 * 1024 * 1024)


def iota(shape, axis):
    return lax.broadcasted_iota(I32, shape, axis)


def onehot(mask):
    return jnp.where(mask, 1.0, 0.0).astype(BF16)


def call(kernel, out, specs, *args):
    return pl.pallas_call(
        kernel,
        out_shape=out,
        in_specs=specs,
        out_specs=jax.tree.map(lambda _: VMEM, out),
        compiler_params=PARAMS,
    )(*args)


def pack_kernel(kept, me, teacher, hidden, packed):
    base = me[0] * SHARD
    count = jnp.int32(0)
    places = [jnp.int32(0)] * MOST
    for j in range(KEPT):
        within = kept[j] - base
        mine = (within >= 0) & (within < SHARD)
        for p in range(MOST):
            places[p] = jnp.where(mine & (count == p), within, places[p])
        count = count + mine.astype(I32)
    rows = NT * R
    picked = jnp.concatenate(
        [teacher[:, pl.ds(pl.multiple_of(w * BLK, BLK), BLK)] for w in places], axis=0
    )
    n = MOST * rows
    o, i = iota((n, n), 0), iota((n, n), 1)
    t, p, r = o // (MOST * R), (o // R) % MOST, o % R
    order = onehot(i == p * rows + t * R + r)
    blocks = jnp.dot(order, picked, preferred_element_type=F32).astype(BF16)
    for m in range(2 * NT):
        packed[m, :TOK] = hidden[:, :BLK]
        packed[m, TOK : 2 * TOK] = hidden[:, BLK:]
        packed[m, 2 * TOK :] = blocks[(m % NT) * 16 : (m % NT + 1) * 16]


def compact_kernel(ylo, kept, slot, arrived, piece):
    n, m = KEPT * R, NT * MOST * R
    o, i = iota((n, m), 0), iota((n, m), 1)
    shard = [(kept[j] * 2341) >> 16 for j in range(KEPT)]
    wanted = jnp.zeros((n, m), I32)
    for j in range(KEPT):
        place = jnp.int32(0)
        for k in range(j):
            place = place + (shard[k] == shard[j]).astype(I32)
        wanted = jnp.where(o // R == slot[j], (shard[j] * MOST + place) * R, wanted)
    order = onehot(i == wanted + o % R)
    sent = jnp.concatenate([arrived[u] for u in range(NT)], axis=0)
    rows = jnp.dot(order, sent, preferred_element_type=F32).astype(BF16)
    for h in range(NH):
        piece[h] = rows


def regroup_kernel(pieces, grouped):
    x = pieces[...].astype(F32)
    rows = jnp.concatenate(
        [x[h, s * R : (s + 1) * R] for s in range(KEPT) for h in range(NH)], axis=0
    ).astype(BF16)
    for k in range(NL):
        grouped[k] = rows


def target_kernel(ylo, mine, me, target, *chosen):
    half = target.shape[1] // 2
    n = 2 * NH * NL * R
    k, j = iota((half, n), 0), iota((half, n), 1)
    core, low, high, r = j // 128, (j // 32) % NL, (j // R) % NH, j % R
    column = (high * NL + low) * 64 + (core ^ mine[0]) * 32 + me[0] * R + r
    order = onehot(k == column)
    for dy in range(2):
        start = pl.multiple_of((ylo[0] ^ dy) * half, half)
        got = jnp.dot(
            target[:, pl.ds(start, half)], order, preferred_element_type=F32
        ).astype(BF16)
        for dc in range(2):
            chosen[2 * dy + dc][...] = got[:, dc * 128 : (dc + 1) * 128]


def main_kernel(ylo, own, other, weights, t0, t1, t2, t3, o0, o1, o2, o3, gradient, full):
    for k in range(NL):
        for s in range(KEPT):
            full[k * 32 : (k + 1) * 32, s * BLK : (s + 1) * BLK] = weights[
                k, s * 32 : (s + 1) * 32, :
            ]
    targets, outs = (t0, t1, t2, t3), (o0, o1, o2, o3)

    def tokens(dy, dc, t):
        block = ((own, other)[dc]).at[(ylo[0] ^ dy) * NT + t]
        return jnp.concatenate([block[:TOK], block[TOK : 2 * TOK]], axis=1)

    residue = []
    for dy in range(2):
        for dc in range(2):
            total = jnp.zeros((TOK, 128), F32)
            for t in range(NT):
                total = total + lax.dot_general(
                    tokens(dy, dc, t),
                    full[:, t * UNITS : (t + 1) * UNITS],
                    (((1,), (1,)), ((), ())),
                    preferred_element_type=F32,
                )
            rounded = total.astype(BF16)
            outs[2 * dy + dc][...] = rounded
            wanted = targets[2 * dy + dc][...]
            residue.append((rounded.astype(F32) - wanted.astype(F32)).astype(BF16))
    for t in range(NT):
        total = jnp.zeros((128, UNITS), F32)
        for dy in range(2):
            for dc in range(2):
                total = total + lax.dot_general(
                    residue[2 * dy + dc],
                    tokens(dy, dc, t),
                    (((0,), (0,)), ((), ())),
                    preferred_element_type=F32,
                )
        total = total.astype(BF16)
        for k in range(NL):
            for s in range(2):
                gradient[k, (2 * t + s) * 32 : (2 * t + s + 1) * 32, :] = total[
                    k * 32 : (k + 1) * 32, s * BLK : (s + 1) * BLK
                ]


def first_sum_kernel(parts, summed):
    total = parts[0].astype(F32)
    for k in range(1, NL):
        total = total + parts[k].astype(F32)
    for h in range(NH):
        summed[h] = jnp.concatenate(
            [total[s * 32 + h * R : s * 32 + (h + 1) * R] for s in range(KEPT)], axis=0
        ).astype(BF16)


def spread_kernel(ylo, mine, p0, p1, p2, p3, blocks):
    parts = (p0, p1, p2, p3)
    k, j = iota((512, 512), 0), iota((512, 512), 1)
    x, half, core, odd, low, r = (
        j // 128,
        (j // 64) % 2,
        (j // 32) % 2,
        (j // 16) % 2,
        (j // R) % NL,
        j % R,
    )
    column = low * 32 + (2 * x + odd) * R + r
    order = onehot(k == (half * 2 + (core ^ mine[0])) * 128 + column)
    for dy in range(2):
        rows = jnp.concatenate(
            [
                parts[2 * dy + dc][h * 96 : (h + 1) * 96, :]
                for h in range(2)
                for dc in range(2)
            ],
            axis=1,
        )
        got = jnp.dot(rows, order, preferred_element_type=F32).astype(BF16)
        for i in range(4):
            blocks[4 * (ylo[0] ^ dy) + i] = got[:, i * 128 : (i + 1) * 128]


def second_sum_kernel(parts, blocks, joined):
    total = parts[0].astype(F32)
    for k in range(1, NH):
        total = total + parts[k].astype(F32)
    high = total.astype(BF16).astype(F32)
    low = total - high
    for u in range(NT):
        rows = slice(u * 8, (u + 1) * 8)
        joined[u, :96] = blocks[u]
        joined[u, 96:] = jnp.concatenate([high[rows], low[rows]], axis=0).astype(BF16)


def last_kernel(factor, parts, out, gradient):
    for t in range(NT):
        both = parts[t, 96:].astype(F32)
        rows = (both[:8] + both[8:]) * factor
        for s in range(2):
            gradient[t * R : (t + 1) * R, s * BLK : (s + 1) * BLK] = rows[
                s * R : (s + 1) * R
            ]
    rows = jnp.concatenate([parts[t, :96] for t in range(NT)], axis=1)
    k, j = iota((1024, 512), 0), iota((1024, 512), 1)
    z, core, t, r = j // 64, (j // 32) % 2, (j // R) % NT, j % R
    lane = t * 128 + core * 32 + z * R + r
    for half in range(2):
        order = onehot(k == lane + half * 64)
        out[half * 96 : (half + 1) * 96, :] = jnp.dot(
            rows, order, preferred_element_type=F32
        ).astype(BF16)


def exchange(x, axes):
    return lax.all_to_all(x, axes, 0, 0)


def swap(x, dy, dc):
    axes = ("ylo", "core")
    perm = [(2 * y + c, 2 * (y ^ dy) + (c ^ dc)) for y in range(2) for c in range(2)]
    return lax.ppermute(x, axes, perm)


def pairs(own, *others):
    return [own] + [swap(x, i // 2, i % 2) for i, x in enumerate(others, 1)]


def body(teacher, kept, slot, hidden, target):
    place = [lax.axis_index(a).astype(I32)[None] for a in ("ylo", "core", TENSOR)]
    shape = jax.ShapeDtypeStruct
    tile = shape((TOK, 128), BF16)

    packed = call(
        pack_kernel,
        shape((16, 400, 128), BF16),
        [SMEM, SMEM, VMEM, VMEM],
        kept,
        place[2],
        teacher,
        hidden,
    )
    plane = exchange(packed, PLANE)
    chosen = call(target_kernel, (tile,) * 4, [SMEM] * 3 + [VMEM], *place, target)

    smem = pl.BlockSpec(memory_space=pltpu.SMEM)
    plane, *chosen = lax.optimization_barrier((plane, *chosen))
    piece = pl.pallas_call(
        compact_kernel,
        out_shape=shape((NH, 64, 128), BF16),
        grid_spec=pltpu.PrefetchScalarGridSpec(
            num_scalar_prefetch=1,
            grid=(1,),
            in_specs=[smem, smem, pl.BlockSpec((NT, 16, 128), lambda i, y: (y[0], 24, 0))],
            out_specs=pl.BlockSpec((NH, 64, 128), lambda i, y: (0, 0, 0)),
        ),
        compiler_params=PARAMS,
    )(place[0], kept, slot, plane)
    pieces = exchange(piece, "zh")
    other = swap(plane, 0, 1)
    wanted = pairs(*chosen)
    pieces, other, *wanted = lax.optimization_barrier((pieces, other, *wanted))
    grouped = call(regroup_kernel, shape((NL, 512, 128), BF16), [VMEM], pieces)
    weights = exchange(grouped, "zl")

    *outs, gradient = pl.pallas_call(
        main_kernel,
        out_shape=(tile,) * 4 + (shape((NL, 512, 128), BF16),),
        in_specs=[SMEM] + [VMEM] * 7,
        out_specs=(VMEM,) * 5,
        scratch_shapes=[pltpu.VMEM((128, KEPT * BLK), BF16)],
        compiler_params=PARAMS,
    )(place[0], plane, other, weights, *wanted)

    parts = exchange(gradient, "zl")
    summed = call(first_sum_kernel, shape((NH, 64, 128), BF16), [VMEM], parts)
    parts = exchange(summed, "zh")
    groups = pairs(*outs)
    blocks = call(
        spread_kernel, shape((NT, 96, 128), BF16), [SMEM] * 2 + [VMEM] * 4, *place[:2], *groups
    )
    joined = call(
        second_sum_kernel, shape((NT, 112, 128), BF16), [VMEM, VMEM], parts, blocks
    )
    parts = exchange(joined, TENSOR)
    factor = 1.0 / math.sqrt(TOK * 128)
    student, grad = call(
        lambda *refs: last_kernel(factor, *refs),
        (shape((TOK, 512), BF16), shape((32, UNITS), F32)),
        [VMEM],
        parts,
    )
    return student, grad


def solution(mesh):
    fine = Mesh(np.asarray(mesh.devices).reshape(SIZES), AXES)
    dp = ("ylo", "zh", "zl", "core")
    placed = (P(dp, TENSOR), P(), P(), P(dp, TENSOR), P(dp, None))
    return jax.shard_map(
        body,
        mesh=fine,
        in_specs=placed,
        out_specs=(P(dp, TENSOR), P(dp, TENSOR)),
        check_vma=False,
    )
```

time: 218 us -> 182 us (0.83)
  the two profiles are of different devices: /device:TPU:32 before, /device:TPU:2 now
where the time goes in v2:
time: 182 us
  starting transfers between devices  66.4 us (36%)
  waiting for transfers between devices  54.4 us (30%)
  blocking collectives  47.3 us (26%)
  Pallas kernels  8.85 us (5%)
  local copies, waits for them, and re-layouts  3.72 us (2%)
    all_to_all x3, starting transfers between devices, exchange(): return lax.all_to_all(x, axes, 0, 0)  49.4 us
    all_to_all x3, waiting for transfers between devices, exchange(): return lax.all_to_all(x, axes, 0, 0)  49.2 us
    all_to_all x3, blocking collectives, exchange(): return lax.all_to_all(x, axes, 0, 0)  47.3 us
    ppermute x7, starting transfers between devices, swap(): return lax.ppermute(x, axes, perm)  17.1 us
    pallas_call x7, Pallas kernels, call(): pl.pallas_call(kernel, out_shape=out, in_specs=specs, out_specs=jax.tree....  5.68 us
    ppermute x7, waiting for transfers between devices, swap(): return lax.ppermute(x, axes, perm)  5.22 us
    unnamed x26, local copies, waits for them, and re-layouts  3.72 us
  transfers between devices with their start and end apart: 10, of which 7 were waited for; matrix products, arithmetic and copies ran while one was open for 0% of the time, Pallas kernels for 2%

profile of v2, /device:TPU:2, one launch (start us, length us, event | category | flops | bytes accessed | tf_op | source)
XLA Modules:
  0.0 181.5 jit_solution(12848689741426822466)
XLA Ops:
  0.6 0.0 copy-start.1
  0.6 0.9 copy-done.1
  1.6 0.0 copy-start.2
  1.6 0.9 copy-done.2
  2.5 0.0 copy-start.5
  2.5 0.7 copy-done.5
  3.1 2.1 %shard_map.68 = bf16[16,400,128]{2,1,0:T(8,128)(2,1)} custom-call(s32[16]{0:T(128)S(1)} %copy-done.5, s32[1]{0:T(128)} %bitcast.1.me, bf16[32,3584]{1,0:T(8,128)(2,1)S(1)} %copy-done.1, bf16[192,256]{1,0:T(8,128)(2,1)S(1)} %copy-done.2), custom_call_target="tpu_custom_call" | custom-call | tf_op jit(solution)/shard_map/pallas_call | solution.py:47
  5.3 0.0 copy-start
  5.3 0.0 copy-start.6
  5.3 0.0 copy-start.7
  5.3 16.8 %all-to-all-start = ((bf16[16,400,128]{2,1,0:T(8,128)(2,1)}), bf16[16,400,128]{2,1,0:T(8,128)(2,1)S(1)}, u32[]{:S(2)}, u32[]{:S(2)}) async-start(bf16[16,400,128]{2,1,0:T(8,128)(2,1)} %shard_map.68), calls=%async_computation | async-start | bytes 3276800 | tf_op jit(solution)/shard_map/all_to_all | solution.py:237
  22.1 0.0 copy-done
  22.1 1.2 shard_map.69
  23.3 0.0 copy-start.8
  23.3 0.0 copy-start.9
  23.3 14.3 %all-to-all-done.arrived.own = bf16[16,400,128]{2,1,0:T(8,128)(2,1)S(1)} async-done(((bf16[16,400,128]{2,1,0:T(8,128)(2,1)}), bf16[16,400,128]{2,1,0:T(8,128)(2,1)S(1)}, u32[]{:S(2)}, u32[]{:S(2)}) %all-to-all-start) | async-done | bytes 1638432 | tf_op jit(solution)/shard_map/all_to_all | solution.py:237
  37.6 0.0 copy-done.8
  37.6 1.9 %collective-permute-start = (bf16[16,400,128]{2,1,0:T(8,128)(2,1)S(1)}, bf16[16,400,128]{2,1,0:T(8,128)(2,1)S(1)}, u32[]{:S(2)}, u32[]{:S(2)}) collective-permute-start(bf16[16,400,128]{2,1,0:T(8,128)(2,1)S(1)} %all-to-all-done.arrived.own), channel_id=1, source_target_pairs={{0,8},{8,0},{512,520},{520,512},{1,9},{9,1},{513,521},{521,513},{2... | collective-permute-start | bytes 4915208 | tf_op jit(solution)/shard_map/ppermute | solution.py:243
  39.5 0.0 copy-done.6
  39.5 0.0 copy-done.7
  39.5 1.5 shard_map.70
  41.0 0.0 copy-done.9
  41.0 26.5 %all-to-all-start.1 = ((bf16[8,64,128]{2,1,0:T(8,128)(2,1)}), bf16[8,64,128]{2,1,0:T(8,128)(2,1)S(1)}, u32[]{:S(2)}, u32[]{:S(2)}) async-start(bf16[8,64,128]{2,1,0:T(8,128)(2,1)} %shard_map.70), calls=%async_computation.1 | async-start | bytes 262144 | tf_op jit(solution)/shard_map/all_to_all | solution.py:237
  67.6 2.1 %collective-permute-start.1 = (bf16[192,128]{1,0:T(8,128)(2,1)}, bf16[192,128]{1,0:T(8,128)(2,1)S(1)}, u32[]{:S(2)}, u32[]{:S(2)}) collective-permute-start(bf16[192,128]{1,0:T(8,128)(2,1)} %get-tuple-element.28), channel_id=1, source_target_pairs={{0,8},{8,0},{512,520},{520,512},{1,9},{9,1},{513,521},{521,513},{2... | collective-permute-start | bytes 147464 | tf_op jit(solution)/shard_map/ppermute | solution.py:243
  69.7 2.4 %collective-permute-start.2 = (bf16[192,128]{1,0:T(8,128)(2,1)}, bf16[192,128]{1,0:T(8,128)(2,1)S(1)}, u32[]{:S(2)}, u32[]{:S(2)}) collective-permute-start(bf16[192,128]{1,0:T(8,128)(2,1)} %copy-done.9), channel_id=1, source_target_pairs={{0,512},{8,520},{512,0},{520,8},{1,513},{9,521},{513,1},{521,9},{2... | collective-permute-start | bytes 147464 | tf_op jit(solution)/shard_map/ppermute | solution.py:243
  72.1 3.1 %collective-permute-start.3 = (bf16[192,128]{1,0:T(8,128)(2,1)}, bf16[192,128]{1,0:T(8,128)(2,1)S(1)}, u32[]{:S(2)}, u32[]{:S(2)}) collective-permute-start(bf16[192,128]{1,0:T(8,128)(2,1)} %copy-done.8), channel_id=1, source_target_pairs={{0,520},{8,512},{512,8},{520,0},{1,521},{9,513},{513,9},{521,1},{2... | collective-permute-start | bytes 147464 | tf_op jit(solution)/shard_map/ppermute | solution.py:243
  75.2 0.0 collective-permute-done.1.t1
  75.2 0.7 collective-permute-done.2.t2
  75.9 2.2 %collective-permute-done.3.t3 = bf16[192,128]{1,0:T(8,128)(2,1)S(1)} collective-permute-done((bf16[192,128]{1,0:T(8,128)(2,1)}, bf16[192,128]{1,0:T(8,128)(2,1)S(1)}, u32[]{:S(2)}, u32[]{:S(2)}) %collective-permute-start.3) | collective-permute-done | bytes 49184 | tf_op jit(solution)/shard_map/ppermute | solution.py:243
  78.0 0.0 copy-start.3
  78.1 0.6 copy-done.3
  78.7 16.7 %all-to-all-done.1.pieces = bf16[8,64,128]{2,1,0:T(8,128)(2,1)S(1)} async-done(((bf16[8,64,128]{2,1,0:T(8,128)(2,1)}), bf16[8,64,128]{2,1,0:T(8,128)(2,1)S(1)}, u32[]{:S(2)}, u32[]{:S(2)}) %all-to-all-start.1) | async-done | bytes 131104 | tf_op jit(solution)/shard_map/all_to_all | solution.py:237
  95.4 0.0 copy-start.4
  95.4 0.0 collective-permute-done.other
  95.4 18.9 %all_to_all.30.weights = bf16[4,512,128]{2,1,0:T(8,128)(2,1)S(1)} all-to-all(bf16[4,512,128]{2,1,0:T(8,128)(2,1)S(1)} %shard_map.71), channel_id=1, replica_groups=mesh['ylo'=2,'zh'=8,'zl'=4,'core'=2,'yhi'=2,'x'=4] {'zl'}, dimensions={0} | all-to-all | bytes 1048576 | tf_op jit(solution)/shard_map/all_to_all | solution.py:237
  114.3 0.0 copy-done.4
  114.3 1.7 shard_map.72
  116.0 0.0 copy-start.11
  116.0 0.6 copy-done.11
  116.6 0.0 copy-start.10
  116.6 0.0 copy-start.12
  116.6 16.0 %all_to_all.31.parts = bf16[4,512,128]{2,1,0:T(8,128)(2,1)S(1)} all-to-all(bf16[4,512,128]{2,1,0:T(8,128)(2,1)S(1)} %get-tuple-element.37), channel_id=1, replica_groups=mesh['ylo'=2,'zh'=8,'zl'=4,'core'=2,'yhi'=2,'x'=4] {'zl'}, dimensions={0} | all-to-all | bytes 1048576 | tf_op jit(solution)/shard_map/all_to_all | solution.py:237
  132.6 0.0 copy-done.10
  132.6 0.7 shard_map.73
  133.3 6.0 %all-to-all-start.4 = ((bf16[8,64,128]{2,1,0:T(8,128)(2,1)}), bf16[8,64,128]{2,1,0:T(8,128)(2,1)S(1)}, u32[]{:S(2)}, u32[]{:S(2)}) async-start(bf16[8,64,128]{2,1,0:T(8,128)(2,1)} %shard_map.73), calls=%async_computation.4 | async-start | bytes 262144 | tf_op jit(solution)/shard_map/all_to_all | solution.py:237
  139.3 0.0 copy-done.12
  139.3 1.9 %collective-permute-start.4 = (bf16[192,128]{1,0:T(8,128)(2,1)S(1)}, bf16[192,128]{1,0:T(8,128)(2,1)S(1)}, u32[]{:S(2)}, u32[]{:S(2)}) collective-permute-start(bf16[192,128]{1,0:T(8,128)(2,1)S(1)} %copy-done.12), channel_id=1, source_target_pairs={{0,8},{8,0},{512,520},{520,512},{1,9},{9,1},{513,521},{521,513},{2... | collective-permute-start | bytes 147464 | tf_op jit(solution)/shard_map/ppermute | solution.py:243
  141.3 2.4 %collective-permute-start.5 = (bf16[192,128]{1,0:T(8,128)(2,1)}, bf16[192,128]{1,0:T(8,128)(2,1)S(1)}, u32[]{:S(2)}, u32[]{:S(2)}) collective-permute-start(bf16[192,128]{1,0:T(8,128)(2,1)} %copy-done.10), channel_id=1, source_target_pairs={{0,512},{8,520},{512,0},{520,8},{1,513},{9,521},{513,1},{521,9},{2... | collective-permute-start | bytes 147464 | tf_op jit(solution)/shard_map/ppermute | solution.py:243
  143.7 3.3 %collective-permute-start.6 = (bf16[192,128]{1,0:T(8,128)(2,1)S(1)}, bf16[192,128]{1,0:T(8,128)(2,1)S(1)}, u32[]{:S(2)}, u32[]{:S(2)}) collective-permute-start(bf16[192,128]{1,0:T(8,128)(2,1)S(1)} %get-tuple-element.41), channel_id=1, source_target_pairs={{0,520},{8,512},{512,8},{520,0},{1,521},{9,513},{513,9},{521,1},{2... | collective-permute-start | bytes 147464 | tf_op jit(solution)/shard_map/ppermute | solution.py:243
  147.0 0.0 collective-permute-done.4.p1
  147.0 0.6 collective-permute-done.5.p2
  147.5 1.8 collective-permute-done.6.p3
  149.3 0.4 shard_map.74.blocks
  149.7 18.2 %all-to-all-done.4.parts = bf16[8,64,128]{2,1,0:T(8,128)(2,1)S(1)} async-done(((bf16[8,64,128]{2,1,0:T(8,128)(2,1)}), bf16[8,64,128]{2,1,0:T(8,128)(2,1)S(1)}, u32[]{:S(2)}, u32[]{:S(2)}) %all-to-all-start.4) | async-done | bytes 131104 | tf_op jit(solution)/shard_map/all_to_all | solution.py:237
  167.9 12.5 %all_to_all.32.refs_0_ = bf16[8,112,128]{2,1,0:T(8,128)(2,1)S(1)} all-to-all(bf16[8,112,128]{2,1,0:T(8,128)(2,1)S(1)} %shard_map.75), channel_id=1, replica_groups=mesh['ylo'=2,'zh'=8,'zl'=4,'core'=2,'yhi'=2,'x'=4] {'yhi','x'}, dimensions={0} | all-to-all | bytes 458752 | tf_op jit(solution)/shard_map/all_to_all | solution.py:237
  180.4 1.2 shard_map.76
  (2 shorter events, 0.1 us)
Async XLA Ops:
  0.6 0.9 copy-start.1
  1.6 0.9 copy-start.2
  2.5 0.7 copy-start.5
  5.3 16.8 %copy-start = (bf16[192,4096]{1,0:T(8,128)(2,1)S(1)}, bf16[192,4096]{1,0:T(8,128)(2,1)}, u32[]{:S(2)}) copy-start(bf16[192,4096]{1,0:T(8,128)(2,1)} %target.1) | copy-start | bytes 4718596
  5.3 34.3 %copy-start.6 = (s32[16]{0:T(128)S(1)}, s32[16]{0:T(128)}, u32[]{:S(2)}) copy-start(s32[16]{0:T(128)} %kept.3) | copy-start | bytes 196
  5.3 34.3 %copy-start.7 = (s32[16]{0:T(128)S(1)}, s32[16]{0:T(128)}, u32[]{:S(2)}) copy-start(s32[16]{0:T(128)} %slot.1) | copy-start | bytes 196
  5.3 32.3 %all-to-all-start = ((bf16[16,400,128]{2,1,0:T(8,128)(2,1)}), bf16[16,400,128]{2,1,0:T(8,128)(2,1)S(1)}, u32[]{:S(2)}, u32[]{:S(2)}) async-start(bf16[16,400,128]{2,1,0:T(8,128)(2,1)} %shard_map.68), calls=%async_computation | async-start | bytes 3276800 | tf_op jit(solution)/shard_map/all_to_all | solution.py:237
  23.3 14.3 %copy-start.8 = (bf16[192,128]{1,0:T(8,128)(2,1)}, bf16[192,128]{1,0:T(8,128)(2,1)S(1)}, u32[]{:S(2)}) copy-start(bf16[192,128]{1,0:T(8,128)(2,1)S(1)} %get-tuple-element.30) | copy-start | bytes 147460
  23.3 17.7 %copy-start.9 = (bf16[192,128]{1,0:T(8,128)(2,1)}, bf16[192,128]{1,0:T(8,128)(2,1)S(1)}, u32[]{:S(2)}) copy-start(bf16[192,128]{1,0:T(8,128)(2,1)S(1)} %get-tuple-element.29) | copy-start | bytes 147460
  37.6 57.8 %collective-permute-start = (bf16[16,400,128]{2,1,0:T(8,128)(2,1)S(1)}, bf16[16,400,128]{2,1,0:T(8,128)(2,1)S(1)}, u32[]{:S(2)}, u32[]{:S(2)}) collective-permute-start(bf16[16,400,128]{2,1,0:T(8,128)(2,1)S(1)} %all-to-all-done.arrived.own), channel_id=1, source_target_pairs={{0,8},{8,0},{512,520},{520,512},{1,9},{9,1},{513,521},{521,513},{2... | collective-permute-start | bytes 4915208 | tf_op jit(solution)/shard_map/ppermute | solution.py:243
  41.0 54.3 %all-to-all-start.1 = ((bf16[8,64,128]{2,1,0:T(8,128)(2,1)}), bf16[8,64,128]{2,1,0:T(8,128)(2,1)S(1)}, u32[]{:S(2)}, u32[]{:S(2)}) async-start(bf16[8,64,128]{2,1,0:T(8,128)(2,1)} %shard_map.70), calls=%async_computation.1 | async-start | bytes 262144 | tf_op jit(solution)/shard_map/all_to_all | solution.py:237
  67.6 7.6 %collective-permute-start.1 = (bf16[192,128]{1,0:T(8,128)(2,1)}, bf16[192,128]{1,0:T(8,128)(2,1)S(1)}, u32[]{:S(2)}, u32[]{:S(2)}) collective-permute-start(bf16[192,128]{1,0:T(8,128)(2,1)} %get-tuple-element.28), channel_id=1, source_target_pairs={{0,8},{8,0},{512,520},{520,512},{1,9},{9,1},{513,521},{521,513},{2... | collective-permute-start | bytes 147464 | tf_op jit(solution)/shard_map/ppermute | solution.py:243
  69.7 6.2 %collective-permute-start.2 = (bf16[192,128]{1,0:T(8,128)(2,1)}, bf16[192,128]{1,0:T(8,128)(2,1)S(1)}, u32[]{:S(2)}, u32[]{:S(2)}) collective-permute-start(bf16[192,128]{1,0:T(8,128)(2,1)} %copy-done.9), channel_id=1, source_target_pairs={{0,512},{8,520},{512,0},{520,8},{1,513},{9,521},{513,1},{521,9},{2... | collective-permute-start | bytes 147464 | tf_op jit(solution)/shard_map/ppermute | solution.py:243
  72.1 6.0 %collective-permute-start.3 = (bf16[192,128]{1,0:T(8,128)(2,1)}, bf16[192,128]{1,0:T(8,128)(2,1)S(1)}, u32[]{:S(2)}, u32[]{:S(2)}) collective-permute-start(bf16[192,128]{1,0:T(8,128)(2,1)} %copy-done.8), channel_id=1, source_target_pairs={{0,520},{8,512},{512,8},{520,0},{1,521},{9,513},{513,9},{521,1},{2... | collective-permute-start | bytes 147464 | tf_op jit(solution)/shard_map/ppermute | solution.py:243
  78.0 0.6 copy-start.3
  95.4 18.9 %copy-start.4 = (bf16[192,128]{1,0:T(8,128)(2,1)S(1)}, bf16[192,128]{1,0:T(8,128)(2,1)}, u32[]{:S(2)}) copy-start(bf16[192,128]{1,0:T(8,128)(2,1)} %copy-done.3) | copy-start | bytes 147460
  116.0 0.6 copy-start.11
  116.6 16.0 %copy-start.10 = (bf16[192,128]{1,0:T(8,128)(2,1)}, bf16[192,128]{1,0:T(8,128)(2,1)S(1)}, u32[]{:S(2)}) copy-start(bf16[192,128]{1,0:T(8,128)(2,1)S(1)} %get-tuple-element.40) | copy-start | bytes 147460
  116.6 22.7 %copy-start.12 = (bf16[192,128]{1,0:T(8,128)(2,1)S(1)}, bf16[192,128]{1,0:T(8,128)(2,1)}, u32[]{:S(2)}) copy-start(bf16[192,128]{1,0:T(8,128)(2,1)} %copy-done.11) | copy-start | bytes 147460
  133.3 34.6 %all-to-all-start.4 = ((bf16[8,64,128]{2,1,0:T(8,128)(2,1)}), bf16[8,64,128]{2,1,0:T(8,128)(2,1)S(1)}, u32[]{:S(2)}, u32[]{:S(2)}) async-start(bf16[8,64,128]{2,1,0:T(8,128)(2,1)} %shard_map.73), calls=%async_computation.4 | async-start | bytes 262144 | tf_op jit(solution)/shard_map/all_to_all | solution.py:237
  139.3 7.6 %collective-permute-start.4 = (bf16[192,128]{1,0:T(8,128)(2,1)S(1)}, bf16[192,128]{1,0:T(8,128)(2,1)S(1)}, u32[]{:S(2)}, u32[]{:S(2)}) collective-permute-start(bf16[192,128]{1,0:T(8,128)(2,1)S(1)} %copy-done.12), channel_id=1, source_target_pairs={{0,8},{8,0},{512,520},{520,512},{1,9},{9,1},{513,521},{521,513},{2... | collective-permute-start | bytes 147464 | tf_op jit(solution)/shard_map/ppermute | solution.py:243
  141.3 6.2 %collective-permute-start.5 = (bf16[192,128]{1,0:T(8,128)(2,1)}, bf16[192,128]{1,0:T(8,128)(2,1)S(1)}, u32[]{:S(2)}, u32[]{:S(2)}) collective-permute-start(bf16[192,128]{1,0:T(8,128)(2,1)} %copy-done.10), channel_id=1, source_target_pairs={{0,512},{8,520},{512,0},{520,8},{1,513},{9,521},{513,1},{521,9},{2... | collective-permute-start | bytes 147464 | tf_op jit(solution)/shard_map/ppermute | solution.py:243
  143.7 5.6 %collective-permute-start.6 = (bf16[192,128]{1,0:T(8,128)(2,1)S(1)}, bf16[192,128]{1,0:T(8,128)(2,1)S(1)}, u32[]{:S(2)}, u32[]{:S(2)}) collective-permute-start(bf16[192,128]{1,0:T(8,128)(2,1)S(1)} %get-tuple-element.41), channel_id=1, source_target_pairs={{0,520},{8,512},{512,8},{520,0},{1,521},{9,513},{513,9},{521,1},{2... | collective-permute-start | bytes 147464 | tf_op jit(solution)/shard_map/ppermute | solution.py:243

commit v3 on v2

--- a/solution.py
+++ b/solution.py
@@ -16,8 +16,6 @@
 AXES = ("ylo", "zh", "zl", "core", "yhi", "x")
 SIZES = (2, 8, 4, 2, 2, 4)
 TENSOR = ("yhi", "x")
-PLANE = ("ylo", "yhi", "x")
-PAIR = ("ylo", "core")
 
 BLK = 128
 KEPT = 16
@@ -25,6 +23,7 @@
 NT = 8
 NH = 8
 NL = 4
+ORDER = tuple((h + NH // 2) % NH for h in range(NH))
 R = 4
 SHARD = 28
 TOK = 192
@@ -72,13 +71,13 @@
     t, p, r = o // (MOST * R), (o // R) % MOST, o % R
     order = onehot(i == p * rows + t * R + r)
     blocks = jnp.dot(order, picked, preferred_element_type=F32).astype(BF16)
-    for m in range(2 * NT):
+    for m in range(NT):
         packed[m, :TOK] = hidden[:, :BLK]
         packed[m, TOK : 2 * TOK] = hidden[:, BLK:]
-        packed[m, 2 * TOK :] = blocks[(m % NT) * 16 : (m % NT + 1) * 16]
-
-
-def compact_kernel(ylo, kept, slot, arrived, piece):
+        packed[m, 2 * TOK :] = blocks[m * 16 : (m + 1) * 16]
+
+
+def compact_kernel(kept, slot, arrived, piece):
     n, m = KEPT * R, NT * MOST * R
     o, i = iota((n, m), 0), iota((n, m), 1)
     shard = [(kept[j] * 2341) >> 16 for j in range(KEPT)]
@@ -98,7 +97,7 @@
 def regroup_kernel(pieces, grouped):
     x = pieces[...].astype(F32)
     rows = jnp.concatenate(
-        [x[h, s * R : (s + 1) * R] for s in range(KEPT) for h in range(NH)], axis=0
+        [x[ORDER.index(h), s * R : (s + 1) * R] for s in range(KEPT) for h in range(NH)], axis=0
     ).astype(BF16)
     for k in range(NL):
         grouped[k] = rows
@@ -120,18 +119,25 @@
             chosen[2 * dy + dc][...] = got[:, dc * 128 : (dc + 1) * 128]
 
 
-def main_kernel(ylo, own, other, weights, t0, t1, t2, t3, o0, o1, o2, o3, gradient, full):
-    for k in range(NL):
-        for s in range(KEPT):
-            full[k * 32 : (k + 1) * 32, s * BLK : (s + 1) * BLK] = weights[
-                k, s * 32 : (s + 1) * 32, :
-            ]
+def main_kernel(h, h1, h3, g, g1, g3, weights, t0, t1, t2, t3, o0, o1, o2, o3, gradient):
+    hidden = (((h, 0, h, 0), (h1, 0, h3, 4)), ((g, 0, g, 0), (g1, 0, g3, 4)))
     targets, outs = (t0, t1, t2, t3), (o0, o1, o2, o3)
 
     def tokens(dy, dc, t):
-        block = ((own, other)[dc]).at[(ylo[0] ^ dy) * NT + t]
-        return jnp.concatenate([block[:TOK], block[TOK : 2 * TOK]], axis=1)
-
+        ref, first = hidden[dc][dy][2 * (t // 4) : 2 * (t // 4) + 2]
+        i = t - first
+        return jnp.concatenate([ref[i, :TOK], ref[i, TOK : 2 * TOK]], axis=1)
+
+    columns = []
+    for t in range(NT):
+        halves = [
+            jnp.concatenate(
+                [weights[k, (2 * t + s) * 32 : (2 * t + s + 1) * 32, :] for k in range(NL)],
+                axis=0,
+            )
+            for s in range(2)
+        ]
+        columns.append(jnp.concatenate(halves, axis=1))
     residue = []
     for dy in range(2):
         for dc in range(2):
@@ -139,7 +145,7 @@
             for t in range(NT):
                 total = total + lax.dot_general(
                     tokens(dy, dc, t),
-                    full[:, t * UNITS : (t + 1) * UNITS],
+                    columns[t],
                     (((1,), (1,)), ((), ())),
                     preferred_element_type=F32,
                 )
@@ -170,7 +176,7 @@
     for k in range(1, NL):
         total = total + parts[k].astype(F32)
     for h in range(NH):
-        summed[h] = jnp.concatenate(
+        summed[ORDER.index(h)] = jnp.concatenate(
             [total[s * 32 + h * R : s * 32 + (h + 1) * R] for s in range(KEPT)], axis=0
         ).astype(BF16)
 
@@ -233,18 +239,18 @@
         ).astype(BF16)
 
 
-def exchange(x, axes):
-    return lax.all_to_all(x, axes, 0, 0)
-
-
-def swap(x, dy, dc):
-    axes = ("ylo", "core")
-    perm = [(2 * y + c, 2 * (y ^ dy) + (c ^ dc)) for y in range(2) for c in range(2)]
-    return lax.ppermute(x, axes, perm)
+def exchange(x, axes, order=None):
+    groups = None if order is None else [list(order)]
+    return lax.all_to_all(x, axes, 0, 0, axis_index_groups=groups)
+
+
+def shift(a, y=0, core=0):
+    bits = ((y & 1) << 2) | (core << 1) | (y >> 1)
+    return lax.ppermute(a, ("ylo", "core", "yhi"), [(i, i ^ bits) for i in range(8)])
 
 
 def pairs(own, *others):
-    return [own] + [swap(x, i // 2, i % 2) for i, x in enumerate(others, 1)]
+    return [own] + [shift(a, y=i // 2, core=i % 2) for i, a in enumerate(others, 1)]
 
 
 def body(teacher, kept, slot, hidden, target):
@@ -254,48 +260,49 @@
 
     packed = call(
         pack_kernel,
-        shape((16, 400, 128), BF16),
+        shape((NT, 400, 128), BF16),
         [SMEM, SMEM, VMEM, VMEM],
         kept,
         place[2],
         teacher,
         hidden,
     )
-    plane = exchange(packed, PLANE)
+    row = exchange(packed, TENSOR)
     chosen = call(target_kernel, (tile,) * 4, [SMEM] * 3 + [VMEM], *place, target)
 
     smem = pl.BlockSpec(memory_space=pltpu.SMEM)
-    plane, *chosen = lax.optimization_barrier((plane, *chosen))
     piece = pl.pallas_call(
         compact_kernel,
         out_shape=shape((NH, 64, 128), BF16),
-        grid_spec=pltpu.PrefetchScalarGridSpec(
-            num_scalar_prefetch=1,
-            grid=(1,),
-            in_specs=[smem, smem, pl.BlockSpec((NT, 16, 128), lambda i, y: (y[0], 24, 0))],
-            out_specs=pl.BlockSpec((NH, 64, 128), lambda i, y: (0, 0, 0)),
-        ),
+        grid=(1,),
+        in_specs=[smem, smem, pl.BlockSpec((NT, 16, 128), lambda i: (0, 24, 0))],
+        out_specs=pl.BlockSpec((NH, 64, 128), lambda i: (0, 0, 0)),
         compiler_params=PARAMS,
-    )(place[0], kept, slot, plane)
-    pieces = exchange(piece, "zh")
-    other = swap(plane, 0, 1)
+    )(kept, slot, row)
+    pieces = exchange(piece, "zh", ORDER)
+    beside = [shift(row[:4], y=1), shift(row[4:], y=3)]
+    swapped = shift(row, core=1)
     wanted = pairs(*chosen)
-    pieces, other, *wanted = lax.optimization_barrier((pieces, other, *wanted))
+    pieces, swapped, beside, wanted = lax.optimization_barrier((pieces, swapped, beside, wanted))
     grouped = call(regroup_kernel, shape((NL, 512, 128), BF16), [VMEM], pieces)
     weights = exchange(grouped, "zl")
-
-    *outs, gradient = pl.pallas_call(
+    others = [shift(a, core=1) for a in beside]
+
+    *outs, gradient = call(
         main_kernel,
-        out_shape=(tile,) * 4 + (shape((NL, 512, 128), BF16),),
-        in_specs=[SMEM] + [VMEM] * 7,
-        out_specs=(VMEM,) * 5,
-        scratch_shapes=[pltpu.VMEM((128, KEPT * BLK), BF16)],
-        compiler_params=PARAMS,
-    )(place[0], plane, other, weights, *wanted)
+        (tile,) * 4 + (shape((NL, 512, 128), BF16),),
+        [VMEM] * 11,
+        row,
+        *beside,
+        swapped,
+        *others,
+        weights,
+        *wanted,
+    )
 
     parts = exchange(gradient, "zl")
     summed = call(first_sum_kernel, shape((NH, 64, 128), BF16), [VMEM], parts)
-    parts = exchange(summed, "zh")
+    parts = exchange(summed, "zh", ORDER)
     groups = pairs(*outs)
     blocks = call(
         spread_kernel, shape((NT, 96, 128), BF16), [SMEM] * 2 + [VMEM] * 4, *place[:2], *groups

time: 182 us -> 170 us (0.934)
  the two profiles are of different devices: /device:TPU:2 before, /device:TPU:1 now
where the time goes in v3:
time: 170 us; the launch traced here: 169 us
  starting transfers between devices  92.2 us (54%)
  blocking collectives  46.9 us (28%)
  waiting for transfers between devices  16.9 us (10%)
  Pallas kernels  8.84 us (5%)
  local copies, waits for them, and re-layouts  3.5 us (2%)
    all_to_all x3, starting transfers between devices, exchange(): return lax.all_to_all(x, axes, 0, 0, axis_index_groups=groups)  61.3 us
    all_to_all x3, blocking collectives, exchange(): return lax.all_to_all(x, axes, 0, 0, axis_index_groups=groups)  46.9 us
    ppermute x11, starting transfers between devices, shift(): lax.ppermute(a, ('ylo', 'core', 'yhi'), [(i, i ^ bits) for i in range(8)])  30.9 us
    all_to_all x3, waiting for transfers between devices, exchange(): return lax.all_to_all(x, axes, 0, 0, axis_index_groups=groups)  8.5 us
    ppermute x11, waiting for transfers between devices, shift(): lax.ppermute(a, ('ylo', 'core', 'yhi'), [(i, i ^ bits) for i in range(8)])  8.37 us
    pallas_call x8, Pallas kernels, call(): pl.pallas_call(kernel, out_shape=out, in_specs=specs, out_specs=jax.tree....  7.35 us
  transfers between devices with their start and end apart: 14, of which 5 were waited for; matrix products, arithmetic and copies ran while one was open for 1% of the time, Pallas kernels for 1%

profile of v3, /device:TPU:1, one launch (start us, length us, event | category | flops | bytes accessed | tf_op | source)
XLA Modules:
  0.0 169.1 jit_solution(14783680064685889143)
XLA Ops:
  0.6 0.0 copy-start.4
  0.6 0.0 copy-start.1
  0.7 0.9 copy-done.1
  1.6 0.0 copy-start.2
  1.6 0.9 copy-done.2
  2.5 0.0 copy-start.3
  2.5 0.7 copy-done.3
  3.1 0.8 shard_map.68
  4.0 18.1 %all_to_all.30.arrived.h = bf16[8,400,128]{2,1,0:T(8,128)(2,1)S(1)} all-to-all(bf16[8,400,128]{2,1,0:T(8,128)(2,1)S(1)} %shard_map.68), channel_id=1, replica_groups=mesh['ylo'=2,'zh'=8,'zl'=4,'core'=2,'yhi'=2,'x'=4] {'yhi','x'}, dimensions={0} | all-to-all | bytes 1638400 | tf_op jit(solution)/shard_map/all_to_all | solution.py:244
  22.1 0.0 copy-done.4
  22.1 0.0 copy-start
  22.1 1.5 shard_map.69
  23.6 36.8 %all-to-all-start.1 = ((bf16[8,64,128]{2,1,0:T(8,128)(2,1)}), bf16[8,64,128]{2,1,0:T(8,128)(2,1)S(1)}, u32[]{:S(2)}, u32[]{:S(2)}) async-start(bf16[8,64,128]{2,1,0:T(8,128)(2,1)} %shard_map.69), calls=%async_computation.1 | async-start | bytes 262144 | tf_op jit(solution)/shard_map/all_to_all | solution.py:244
  60.3 4.6 %collective-permute-start = (bf16[8,400,128]{2,1,0:T(8,128)(2,1)S(1)}, bf16[8,400,128]{2,1,0:T(8,128)(2,1)S(1)}, u32[]{:S(2)}, u32[]{:S(2)}) collective-permute-start(bf16[8,400,128]{2,1,0:T(8,128)(2,1)S(1)} %all_to_all.30.arrived.h), channel_id=1, source_target_pairs={{0,8},{4,12},{8,0},{12,4},{512,520},{516,524},{520,512},{524,516},... | collective-permute-start | bytes 2457608 | tf_op jit(solution)/shard_map/ppermute | solution.py:249
  64.9 1.0 fusion
  66.0 2.0 %collective-permute-start.2 = (bf16[4,400,128]{2,1,0:T(8,128)(2,1)}, bf16[4,400,128]{2,1,0:T(8,128)(2,1)}, u32[]{:S(2)}, u32[]{:S(2)}) collective-permute-start(bf16[4,400,128]{2,1,0:T(8,128)(2,1)} %get-tuple-element.36), channel_id=1, source_target_pairs={{0,516},{4,512},{8,524},{12,520},{512,4},{516,0},{520,12},{524,8},... | collective-permute-start | bytes 1228808 | tf_op jit(solution)/shard_map/ppermute | solution.py:249
  68.0 2.2 %collective-permute-start.1 = (bf16[4,400,128]{2,1,0:T(8,128)(2,1)}, bf16[4,400,128]{2,1,0:T(8,128)(2,1)}, u32[]{:S(2)}, u32[]{:S(2)}) collective-permute-start(bf16[4,400,128]{2,1,0:T(8,128)(2,1)} %get-tuple-element.37), channel_id=1, source_target_pairs={{0,512},{4,516},{8,520},{12,524},{512,0},{516,4},{520,8},{524,12},... | collective-permute-start | bytes 1228808 | tf_op jit(solution)/shard_map/ppermute | solution.py:249
  70.2 0.0 copy-done
  70.2 0.6 shard_map.70
  70.8 2.2 %collective-permute-start.3 = (bf16[192,128]{1,0:T(8,128)(2,1)S(1)}, bf16[192,128]{1,0:T(8,128)(2,1)S(1)}, u32[]{:S(2)}, u32[]{:S(2)}) collective-permute-start(bf16[192,128]{1,0:T(8,128)(2,1)S(1)} %get-tuple-element.20), channel_id=1, source_target_pairs={{0,8},{4,12},{8,0},{12,4},{512,520},{516,524},{520,512},{524,516},... | collective-permute-start | bytes 147464 | tf_op jit(solution)/shard_map/ppermute | solution.py:249
  73.0 3.3 %collective-permute-start.4 = (bf16[192,128]{1,0:T(8,128)(2,1)S(1)}, bf16[192,128]{1,0:T(8,128)(2,1)S(1)}, u32[]{:S(2)}, u32[]{:S(2)}) collective-permute-start(bf16[192,128]{1,0:T(8,128)(2,1)S(1)} %get-tuple-element.21), channel_id=1, source_target_pairs={{0,512},{4,516},{8,520},{12,524},{512,0},{516,4},{520,8},{524,12},... | collective-permute-start | bytes 147464 | tf_op jit(solution)/shard_map/ppermute | solution.py:249
  76.4 0.0 collective-permute-done.3.t1
  76.4 2.3 %collective-permute-start.5 = (bf16[192,128]{1,0:T(8,128)(2,1)S(1)}, bf16[192,128]{1,0:T(8,128)(2,1)S(1)}, u32[]{:S(2)}, u32[]{:S(2)}) collective-permute-start(bf16[192,128]{1,0:T(8,128)(2,1)S(1)} %get-tuple-element.22), channel_id=1, source_target_pairs={{0,520},{4,524},{8,512},{12,516},{512,8},{516,12},{520,0},{524,4},... | collective-permute-start | bytes 147464 | tf_op jit(solution)/shard_map/ppermute | solution.py:249
  78.7 3.3 %collective-permute-done.4.t2 = bf16[192,128]{1,0:T(8,128)(2,1)S(1)} collective-permute-done((bf16[192,128]{1,0:T(8,128)(2,1)S(1)}, bf16[192,128]{1,0:T(8,128)(2,1)S(1)}, u32[]{:S(2)}, u32[]{:S(2)}) %collective-permute-start.4) | collective-permute-done | bytes 49184 | tf_op jit(solution)/shard_map/ppermute | solution.py:249
  82.0 1.4 collective-permute-done.5.t3
  83.4 0.0 collective-permute-done.2.h3
  83.4 0.0 collective-permute-done.1.h1
  83.4 0.0 collective-permute-done.g
  83.4 0.0 all-to-all-done.1.pieces
  83.4 0.9 shard_map.71
  84.3 3.5 %all-to-all-start.2 = ((bf16[4,512,128]{2,1,0:T(8,128)(2,1)}), bf16[4,512,128]{2,1,0:T(8,128)(2,1)S(1)}, u32[]{:S(2)}, u32[]{:S(2)}) async-start(bf16[4,512,128]{2,1,0:T(8,128)(2,1)} %shard_map.71), calls=%async_computation.2 | async-start | bytes 1048576 | tf_op jit(solution)/shard_map/all_to_all | solution.py:244
  87.7 2.1 %collective-permute-start.6 = (bf16[4,400,128]{2,1,0:T(8,128)(2,1)}, bf16[4,400,128]{2,1,0:T(8,128)(2,1)S(1)}, u32[]{:S(2)}, u32[]{:S(2)}) collective-permute-start(bf16[4,400,128]{2,1,0:T(8,128)(2,1)} %collective-permute-done.1.h1), channel_id=1, source_target_pairs={{0,8},{4,12},{8,0},{12,4},{512,520},{516,524},{520,512},{524,516},... | collective-permute-start | bytes 1228808 | tf_op jit(solution)/shard_map/ppermute | solution.py:249
  89.8 2.2 %collective-permute-start.7 = (bf16[4,400,128]{2,1,0:T(8,128)(2,1)}, bf16[4,400,128]{2,1,0:T(8,128)(2,1)S(1)}, u32[]{:S(2)}, u32[]{:S(2)}) collective-permute-start(bf16[4,400,128]{2,1,0:T(8,128)(2,1)} %collective-permute-done.2.h3), channel_id=1, source_target_pairs={{0,8},{4,12},{8,0},{12,4},{512,520},{516,524},{520,512},{524,516},... | collective-permute-start | bytes 1228808 | tf_op jit(solution)/shard_map/ppermute | solution.py:249
  92.1 0.0 collective-permute-done.6.g1
  92.1 1.6 collective-permute-done.7.g3
  93.7 8.5 %all-to-all-done.2.weights = bf16[4,512,128]{2,1,0:T(8,128)(2,1)S(1)} async-done(((bf16[4,512,128]{2,1,0:T(8,128)(2,1)}), bf16[4,512,128]{2,1,0:T(8,128)(2,1)S(1)}, u32[]{:S(2)}, u32[]{:S(2)}) %all-to-all-start.2) | async-done | bytes 524320 | tf_op jit(solution)/shard_map/all_to_all | solution.py:244
  102.2 2.8 %shard_map.72 = (bf16[192,128]{1,0:T(8,128)(2,1)S(1)}, bf16[192,128]{1,0:T(8,128)(2,1)S(1)}, bf16[192,128]{1,0:T(8,128)(2,1)S(1)}, bf16[192,128]{1,0:T(8,128)(2,1)S(1)}, bf16[4,512,128]{2,1,0:T(8,128)(2,1)S(1)}) custom-call(bf16[8,400,128]{2,1,0:T(8,128)(2,1)S(1)} %all_to_all.30.arrived.h, bf16[4,400,128]{2,1,0:T(8,128)(2,1)} %collective-permute-done.1.h1, ...), custom_call_target="tpu_custom_call" | custom-call | tf_op jit(solution)/shard_map/pallas_call | solution.py:46
  104.9 15.9 %all_to_all.31.parts = bf16[4,512,128]{2,1,0:T(8,128)(2,1)S(1)} all-to-all(bf16[4,512,128]{2,1,0:T(8,128)(2,1)S(1)} %get-tuple-element.31), channel_id=1, replica_groups=mesh['ylo'=2,'zh'=8,'zl'=4,'core'=2,'yhi'=2,'x'=4] {'zl'}, dimensions={0} | all-to-all | bytes 1048576 | tf_op jit(solution)/shard_map/all_to_all | solution.py:244
  120.9 0.7 shard_map.73
  121.6 21.1 %all-to-all-start.4 = ((bf16[8,64,128]{2,1,0:T(8,128)(2,1)}), bf16[8,64,128]{2,1,0:T(8,128)(2,1)S(1)}, u32[]{:S(2)}, u32[]{:S(2)}) async-start(bf16[8,64,128]{2,1,0:T(8,128)(2,1)} %shard_map.73), calls=%async_computation.4 | async-start | bytes 262144 | tf_op jit(solution)/shard_map/all_to_all | solution.py:244
  142.7 4.4 %collective-permute-start.8 = (bf16[192,128]{1,0:T(8,128)(2,1)S(1)}, bf16[192,128]{1,0:T(8,128)(2,1)S(1)}, u32[]{:S(2)}, u32[]{:S(2)}) collective-permute-start(bf16[192,128]{1,0:T(8,128)(2,1)S(1)} %get-tuple-element.33), channel_id=1, source_target_pairs={{0,8},{4,12},{8,0},{12,4},{512,520},{516,524},{520,512},{524,516},... | collective-permute-start | bytes 147464 | tf_op jit(solution)/shard_map/ppermute | solution.py:249
  147.1 2.1 %collective-permute-start.9 = (bf16[192,128]{1,0:T(8,128)(2,1)S(1)}, bf16[192,128]{1,0:T(8,128)(2,1)S(1)}, u32[]{:S(2)}, u32[]{:S(2)}) collective-permute-start(bf16[192,128]{1,0:T(8,128)(2,1)S(1)} %get-tuple-element.34), channel_id=1, source_target_pairs={{0,512},{4,516},{8,520},{12,524},{512,0},{516,4},{520,8},{524,12},... | collective-permute-start | bytes 147464 | tf_op jit(solution)/shard_map/ppermute | solution.py:249
  149.1 3.4 %collective-permute-start.10 = (bf16[192,128]{1,0:T(8,128)(2,1)S(1)}, bf16[192,128]{1,0:T(8,128)(2,1)S(1)}, u32[]{:S(2)}, u32[]{:S(2)}) collective-permute-start(bf16[192,128]{1,0:T(8,128)(2,1)S(1)} %get-tuple-element.35), channel_id=1, source_target_pairs={{0,520},{4,524},{8,512},{12,516},{512,8},{516,12},{520,0},{524,4},... | collective-permute-start | bytes 147464 | tf_op jit(solution)/shard_map/ppermute | solution.py:249
  152.5 0.0 collective-permute-done.8.p1
  152.6 0.0 collective-permute-done.9.p2
  152.6 2.1 %collective-permute-done.10.p3 = bf16[192,128]{1,0:T(8,128)(2,1)S(1)} collective-permute-done((bf16[192,128]{1,0:T(8,128)(2,1)S(1)}, bf16[192,128]{1,0:T(8,128)(2,1)S(1)}, u32[]{:S(2)}, u32[]{:S(2)}) %collective-permute-start.10) | collective-permute-done | bytes 49184 | tf_op jit(solution)/shard_map/ppermute | solution.py:249
  154.7 0.4 shard_map.74.blocks
  155.1 0.0 all-to-all-done.4.parts
  155.1 12.9 %all_to_all.32.refs_0_ = bf16[8,112,128]{2,1,0:T(8,128)(2,1)S(1)} all-to-all(bf16[8,112,128]{2,1,0:T(8,128)(2,1)S(1)} %shard_map.75), channel_id=1, replica_groups=mesh['ylo'=2,'zh'=8,'zl'=4,'core'=2,'yhi'=2,'x'=4] {'yhi','x'}, dimensions={0} | all-to-all | bytes 458752 | tf_op jit(solution)/shard_map/all_to_all | solution.py:244
  168.0 1.2 shard_map.76
  (1 shorter events, 0.0 us)
Async XLA Ops:
  0.6 21.4 %copy-start.4 = (s32[16]{0:T(128)S(1)}, s32[16]{0:T(128)}, u32[]{:S(2)}) copy-start(s32[16]{0:T(128)} %slot.1) | copy-start | bytes 196
  0.6 0.9 copy-start.1
  1.6 0.9 copy-start.2
  2.5 0.7 copy-start.3
  22.1 48.1 %copy-start = (bf16[192,4096]{1,0:T(8,128)(2,1)S(1)}, bf16[192,4096]{1,0:T(8,128)(2,1)}, u32[]{:S(2)}) copy-start(bf16[192,4096]{1,0:T(8,128)(2,1)} %target.1) | copy-start | bytes 4718596
  23.6 59.8 %all-to-all-start.1 = ((bf16[8,64,128]{2,1,0:T(8,128)(2,1)}), bf16[8,64,128]{2,1,0:T(8,128)(2,1)S(1)}, u32[]{:S(2)}, u32[]{:S(2)}) async-start(bf16[8,64,128]{2,1,0:T(8,128)(2,1)} %shard_map.69), calls=%async_computation.1 | async-start | bytes 262144 | tf_op jit(solution)/shard_map/all_to_all | solution.py:244
  60.3 23.0 %collective-permute-start = (bf16[8,400,128]{2,1,0:T(8,128)(2,1)S(1)}, bf16[8,400,128]{2,1,0:T(8,128)(2,1)S(1)}, u32[]{:S(2)}, u32[]{:S(2)}) collective-permute-start(bf16[8,400,128]{2,1,0:T(8,128)(2,1)S(1)} %all_to_all.30.arrived.h), channel_id=1, source_target_pairs={{0,8},{4,12},{8,0},{12,4},{512,520},{516,524},{520,512},{524,516},... | collective-permute-start | bytes 2457608 | tf_op jit(solution)/shard_map/ppermute | solution.py:249
  66.0 17.4 %collective-permute-start.2 = (bf16[4,400,128]{2,1,0:T(8,128)(2,1)}, bf16[4,400,128]{2,1,0:T(8,128)(2,1)}, u32[]{:S(2)}, u32[]{:S(2)}) collective-permute-start(bf16[4,400,128]{2,1,0:T(8,128)(2,1)} %get-tuple-element.36), channel_id=1, source_target_pairs={{0,516},{4,512},{8,524},{12,520},{512,4},{516,0},{520,12},{524,8},... | collective-permute-start | bytes 1228808 | tf_op jit(solution)/shard_map/ppermute | solution.py:249
  68.0 15.4 %collective-permute-start.1 = (bf16[4,400,128]{2,1,0:T(8,128)(2,1)}, bf16[4,400,128]{2,1,0:T(8,128)(2,1)}, u32[]{:S(2)}, u32[]{:S(2)}) collective-permute-start(bf16[4,400,128]{2,1,0:T(8,128)(2,1)} %get-tuple-element.37), channel_id=1, source_target_pairs={{0,512},{4,516},{8,520},{12,524},{512,0},{516,4},{520,8},{524,12},... | collective-permute-start | bytes 1228808 | tf_op jit(solution)/shard_map/ppermute | solution.py:249
  70.8 5.6 %collective-permute-start.3 = (bf16[192,128]{1,0:T(8,128)(2,1)S(1)}, bf16[192,128]{1,0:T(8,128)(2,1)S(1)}, u32[]{:S(2)}, u32[]{:S(2)}) collective-permute-start(bf16[192,128]{1,0:T(8,128)(2,1)S(1)} %get-tuple-element.20), channel_id=1, source_target_pairs={{0,8},{4,12},{8,0},{12,4},{512,520},{516,524},{520,512},{524,516},... | collective-permute-start | bytes 147464 | tf_op jit(solution)/shard_map/ppermute | solution.py:249
  73.0 9.0 %collective-permute-start.4 = (bf16[192,128]{1,0:T(8,128)(2,1)S(1)}, bf16[192,128]{1,0:T(8,128)(2,1)S(1)}, u32[]{:S(2)}, u32[]{:S(2)}) collective-permute-start(bf16[192,128]{1,0:T(8,128)(2,1)S(1)} %get-tuple-element.21), channel_id=1, source_target_pairs={{0,512},{4,516},{8,520},{12,524},{512,0},{516,4},{520,8},{524,12},... | collective-permute-start | bytes 147464 | tf_op jit(solution)/shard_map/ppermute | solution.py:249
  76.4 7.0 %collective-permute-start.5 = (bf16[192,128]{1,0:T(8,128)(2,1)S(1)}, bf16[192,128]{1,0:T(8,128)(2,1)S(1)}, u32[]{:S(2)}, u32[]{:S(2)}) collective-permute-start(bf16[192,128]{1,0:T(8,128)(2,1)S(1)} %get-tuple-element.22), channel_id=1, source_target_pairs={{0,520},{4,524},{8,512},{12,516},{512,8},{516,12},{520,0},{524,4},... | collective-permute-start | bytes 147464 | tf_op jit(solution)/shard_map/ppermute | solution.py:249
  84.3 17.9 %all-to-all-start.2 = ((bf16[4,512,128]{2,1,0:T(8,128)(2,1)}), bf16[4,512,128]{2,1,0:T(8,128)(2,1)S(1)}, u32[]{:S(2)}, u32[]{:S(2)}) async-start(bf16[4,512,128]{2,1,0:T(8,128)(2,1)} %shard_map.71), calls=%async_computation.2 | async-start | bytes 1048576 | tf_op jit(solution)/shard_map/all_to_all | solution.py:244
  87.7 4.3 %collective-permute-start.6 = (bf16[4,400,128]{2,1,0:T(8,128)(2,1)}, bf16[4,400,128]{2,1,0:T(8,128)(2,1)S(1)}, u32[]{:S(2)}, u32[]{:S(2)}) collective-permute-start(bf16[4,400,128]{2,1,0:T(8,128)(2,1)} %collective-permute-done.1.h1), channel_id=1, source_target_pairs={{0,8},{4,12},{8,0},{12,4},{512,520},{516,524},{520,512},{524,516},... | collective-permute-start | bytes 1228808 | tf_op jit(solution)/shard_map/ppermute | solution.py:249
  89.8 3.9 %collective-permute-start.7 = (bf16[4,400,128]{2,1,0:T(8,128)(2,1)}, bf16[4,400,128]{2,1,0:T(8,128)(2,1)S(1)}, u32[]{:S(2)}, u32[]{:S(2)}) collective-permute-start(bf16[4,400,128]{2,1,0:T(8,128)(2,1)} %collective-permute-done.2.h3), channel_id=1, source_target_pairs={{0,8},{4,12},{8,0},{12,4},{512,520},{516,524},{520,512},{524,516},... | collective-permute-start | bytes 1228808 | tf_op jit(solution)/shard_map/ppermute | solution.py:249
  121.6 33.5 %all-to-all-start.4 = ((bf16[8,64,128]{2,1,0:T(8,128)(2,1)}), bf16[8,64,128]{2,1,0:T(8,128)(2,1)S(1)}, u32[]{:S(2)}, u32[]{:S(2)}) async-start(bf16[8,64,128]{2,1,0:T(8,128)(2,1)} %shard_map.73), calls=%async_computation.4 | async-start | bytes 262144 | tf_op jit(solution)/shard_map/all_to_all | solution.py:244
  142.7 9.9 %collective-permute-start.8 = (bf16[192,128]{1,0:T(8,128)(2,1)S(1)}, bf16[192,128]{1,0:T(8,128)(2,1)S(1)}, u32[]{:S(2)}, u32[]{:S(2)}) collective-permute-start(bf16[192,128]{1,0:T(8,128)(2,1)S(1)} %get-tuple-element.33), channel_id=1, source_target_pairs={{0,8},{4,12},{8,0},{12,4},{512,520},{516,524},{520,512},{524,516},... | collective-permute-start | bytes 147464 | tf_op jit(solution)/shard_map/ppermute | solution.py:249
  147.1 5.5 %collective-permute-start.9 = (bf16[192,128]{1,0:T(8,128)(2,1)S(1)}, bf16[192,128]{1,0:T(8,128)(2,1)S(1)}, u32[]{:S(2)}, u32[]{:S(2)}) collective-permute-start(bf16[192,128]{1,0:T(8,128)(2,1)S(1)} %get-tuple-element.34), channel_id=1, source_target_pairs={{0,512},{4,516},{8,520},{12,524},{512,0},{516,4},{520,8},{524,12},... | collective-permute-start | bytes 147464 | tf_op jit(solution)/shard_map/ppermute | solution.py:249
  149.1 5.5 %collective-permute-start.10 = (bf16[192,128]{1,0:T(8,128)(2,1)S(1)}, bf16[192,128]{1,0:T(8,128)(2,1)S(1)}, u32[]{:S(2)}, u32[]{:S(2)}) collective-permute-start(bf16[192,128]{1,0:T(8,128)(2,1)S(1)} %get-tuple-element.35), channel_id=1, source_target_pairs={{0,520},{4,524},{8,512},{12,516},{512,8},{516,12},{520,0},{524,4},... | collective-permute-start | bytes 147464 | tf_op jit(solution)/shard_map/ppermute | solution.py:249

commit v4 on v3

--- a/solution.py
+++ b/solution.py
@@ -23,7 +23,8 @@
 NT = 8
 NH = 8
 NL = 4
-ORDER = tuple((h + NH // 2) % NH for h in range(NH))
+GATHER = tuple((h + 5) % NH for h in range(NH))
+SCATTER = tuple((h + 4) % NH for h in range(NH))
 R = 4
 SHARD = 28
 TOK = 192
@@ -32,6 +33,7 @@
 VMEM = pl.BlockSpec(memory_space=pltpu.VMEM)
 SMEM = pl.BlockSpec(memory_space=pltpu.SMEM)
 PARAMS = pltpu.CompilerParams(vmem_limit_bytes=40 * 1024 * 1024)
+WHOLE = pltpu.CompilerParams(vmem_limit_bytes=60 * 1024 * 1024)
 
 
 def iota(shape, axis):
@@ -42,13 +44,13 @@
     return jnp.where(mask, 1.0, 0.0).astype(BF16)
 
 
-def call(kernel, out, specs, *args):
+def call(kernel, out, specs, *args, params=PARAMS):
     return pl.pallas_call(
         kernel,
         out_shape=out,
         in_specs=specs,
         out_specs=jax.tree.map(lambda _: VMEM, out),
-        compiler_params=PARAMS,
+        compiler_params=params,
     )(*args)
 
 
@@ -97,7 +99,7 @@
 def regroup_kernel(pieces, grouped):
     x = pieces[...].astype(F32)
     rows = jnp.concatenate(
-        [x[ORDER.index(h), s * R : (s + 1) * R] for s in range(KEPT) for h in range(NH)], axis=0
+        [x[GATHER.index(h), s * R : (s + 1) * R] for s in range(KEPT) for h in range(NH)], axis=0
     ).astype(BF16)
     for k in range(NL):
         grouped[k] = rows
@@ -176,7 +178,7 @@
     for k in range(1, NL):
         total = total + parts[k].astype(F32)
     for h in range(NH):
-        summed[ORDER.index(h)] = jnp.concatenate(
+        summed[SCATTER.index(h)] = jnp.concatenate(
             [total[s * 32 + h * R : s * 32 + (h + 1) * R] for s in range(KEPT)], axis=0
         ).astype(BF16)
 
@@ -244,6 +246,15 @@
     return lax.all_to_all(x, axes, 0, 0, axis_index_groups=groups)
 
 
+def exchange_near(x):
+    groups = []
+    for start in range(0, NH * NL, NL):
+        for core in range(2):
+            members = [(start + 2 * core + i) % (NH * NL) for i in range(NL)]
+            groups.append([2 * z + core for z in sorted(members, key=lambda z: z % NL)])
+    return lax.all_to_all(x, ("zh", "zl", "core"), 0, 0, axis_index_groups=groups)
+
+
 def shift(a, y=0, core=0):
     bits = ((y & 1) << 2) | (core << 1) | (y >> 1)
     return lax.ppermute(a, ("ylo", "core", "yhi"), [(i, i ^ bits) for i in range(8)])
@@ -266,9 +277,12 @@
         place[2],
         teacher,
         hidden,
+        params=WHOLE,
     )
     row = exchange(packed, TENSOR)
     chosen = call(target_kernel, (tile,) * 4, [SMEM] * 3 + [VMEM], *place, target)
+    targets = pairs(*chosen)
+    row, targets = lax.optimization_barrier((row, targets))
 
     smem = pl.BlockSpec(memory_space=pltpu.SMEM)
     piece = pl.pallas_call(
@@ -279,14 +293,12 @@
         out_specs=pl.BlockSpec((NH, 64, 128), lambda i: (0, 0, 0)),
         compiler_params=PARAMS,
     )(kept, slot, row)
-    pieces = exchange(piece, "zh", ORDER)
+    pieces = exchange(piece, "zh", GATHER)
     beside = [shift(row[:4], y=1), shift(row[4:], y=3)]
-    swapped = shift(row, core=1)
-    wanted = pairs(*chosen)
-    pieces, swapped, beside, wanted = lax.optimization_barrier((pieces, swapped, beside, wanted))
+    pieces, beside = lax.optimization_barrier((pieces, beside))
     grouped = call(regroup_kernel, shape((NL, 512, 128), BF16), [VMEM], pieces)
-    weights = exchange(grouped, "zl")
-    others = [shift(a, core=1) for a in beside]
+    weights = exchange_near(grouped)
+    others = [shift(a, core=1) for a in (row, *beside)]
 
     *outs, gradient = call(
         main_kernel,
@@ -294,15 +306,14 @@
         [VMEM] * 11,
         row,
         *beside,
-        swapped,
         *others,
         weights,
-        *wanted,
-    )
-
-    parts = exchange(gradient, "zl")
+        *targets,
+    )
+
+    parts = exchange_near(gradient)
     summed = call(first_sum_kernel, shape((NH, 64, 128), BF16), [VMEM], parts)
-    parts = exchange(summed, "zh", ORDER)
+    parts = exchange(summed, "zh", SCATTER)
     groups = pairs(*outs)
     blocks = call(
         spread_kernel, shape((NT, 96, 128), BF16), [SMEM] * 2 + [VMEM] * 4, *place[:2], *groups

time: 170 us -> 158 us (0.929)
  blocking collectives: 46.9 us -> 30.8 us
  starting transfers between devices: 92.2 us -> 96.3 us
    all_to_all x3 -> x1, blocking collectives: 46.9 us -> 12 us  [exchange(): return lax.all_to_all(x, axes, 0, 0, axis_index_groups=groups)]
    all_to_all x0 -> x1, blocking collectives: none -> 18.9 us  [exchange_near(): lax.all_to_all(x, ('zh', 'zl', 'core'), 0, 0, axis_index_groups=groups)]
    ppermute x11, starting transfers between devices: 30.9 us -> 40.5 us  [shift(): lax.ppermute(a, ('ylo', 'core', 'yhi'), [(i, i ^ bits) for i in range(8)])]
    all_to_all x3, starting transfers between devices: 61.3 us -> 52.4 us  [exchange(): return lax.all_to_all(x, axes, 0, 0, axis_index_groups=groups)]
    all_to_all x3, waiting for transfers between devices: 8.5 us -> 0.15 us  [exchange(): return lax.all_to_all(x, axes, 0, 0, axis_index_groups=groups)]
    ppermute x11, waiting for transfers between devices: 8.37 us -> 15.7 us  [shift(): lax.ppermute(a, ('ylo', 'core', 'yhi'), [(i, i ^ bits) for i in range(8)])]
    all_to_all x0 -> x1, starting transfers between devices: none -> 3.47 us  [exchange_near(): lax.all_to_all(x, ('zh', 'zl', 'core'), 0, 0, axis_index_groups=groups)]
    unnamed x10 -> x26, local copies, waits for them, and re-layouts: 2.49 us -> 4 us
  transfers between devices with their start and end apart: 14 -> 15, of which waited for: 5 -> 6; matrix products, arithmetic and copies ran while one was open for 1% -> 0% of each run, Pallas kernels for 1% -> 1%
where the time goes in v4:
time: 158 us; the launch traced here: 157 us
  starting transfers between devices  96.3 us (61%)
  blocking collectives  30.8 us (19%)
  waiting for transfers between devices  15.8 us (10%)
  Pallas kernels  9.18 us (6%)
  local copies, waits for them, and re-layouts  4.05 us (3%)
    all_to_all x3, starting transfers between devices, exchange(): return lax.all_to_all(x, axes, 0, 0, axis_index_groups=groups)  52.4 us
    ppermute x11, starting transfers between devices, shift(): lax.ppermute(a, ('ylo', 'core', 'yhi'), [(i, i ^ bits) for i in range(8)])  40.5 us
    all_to_all x1, blocking collectives, exchange_near(): lax.all_to_all(x, ('zh', 'zl', 'core'), 0, 0, axis_index_groups=groups)  18.9 us
    ppermute x11, waiting for transfers between devices, shift(): lax.ppermute(a, ('ylo', 'core', 'yhi'), [(i, i ^ bits) for i in range(8)])  15.7 us
    all_to_all x1, blocking collectives, exchange(): return lax.all_to_all(x, axes, 0, 0, axis_index_groups=groups)  12 us
    pallas_call x8, Pallas kernels, call(): pl.pallas_call(kernel, out_shape=out, in_specs=specs, out_specs=jax.tree....  7.69 us
    unnamed x26, local copies, waits for them, and re-layouts  4 us
    all_to_all x1, starting transfers between devices, exchange_near(): lax.all_to_all(x, ('zh', 'zl', 'core'), 0, 0, axis_index_groups=groups)  3.47 us
  transfers between devices with their start and end apart: 15, of which 6 were waited for; matrix products, arithmetic and copies ran while one was open for 0% of the time, Pallas kernels for 1%

profile of v4, /device:TPU:1, one launch (start us, length us, event | category | flops | bytes accessed | tf_op | source)
XLA Modules:
  0.0 157.1 jit_solution(6038987847285982437)
XLA Ops:
  0.6 0.0 copy-start
  0.6 2.3 %shard_map.68 = bf16[8,400,128]{2,1,0:T(8,128)(2,1)} custom-call(s32[16]{0:T(128)} %kept.3, s32[1]{0:T(128)} %bitcast.me, bf16[32,3584]{1,0:T(8,128)(2,1)} %teacher.1, bf16[192,256]{1,0:T(8,128)(2,1)} %hidden.1), custom_call_target="tpu_custom_call" | custom-call | tf_op jit(solution)/shard_map/pallas_call | solution.py:48
  3.0 0.0 copy-start.7
  3.0 0.0 copy-start.8
  3.0 7.6 %all-to-all-start = ((bf16[8,400,128]{2,1,0:T(8,128)(2,1)}), bf16[8,400,128]{2,1,0:T(8,128)(2,1)S(1)}, u32[]{:S(2)}, u32[]{:S(2)}) async-start(bf16[8,400,128]{2,1,0:T(8,128)(2,1)} %shard_map.68), calls=%async_computation | async-start | bytes 1638400 | tf_op jit(solution)/shard_map/all_to_all | solution.py:246
  10.6 0.0 copy-done
  10.6 0.6 shard_map.69
  11.2 12.1 %collective-permute-start = (bf16[192,128]{1,0:T(8,128)(2,1)S(1)}, bf16[192,128]{1,0:T(8,128)(2,1)S(1)}, u32[]{:S(2)}, u32[]{:S(2)}) collective-permute-start(bf16[192,128]{1,0:T(8,128)(2,1)S(1)} %get-tuple-element.20), channel_id=1, source_target_pairs={{0,8},{4,12},{8,0},{12,4},{512,520},{516,524},{520,512},{524,516},... | collective-permute-start | bytes 147464 | tf_op jit(solution)/shard_map/ppermute | solution.py:260
  23.4 1.9 %collective-permute-start.1 = (bf16[192,128]{1,0:T(8,128)(2,1)S(1)}, bf16[192,128]{1,0:T(8,128)(2,1)S(1)}, u32[]{:S(2)}, u32[]{:S(2)}) collective-permute-start(bf16[192,128]{1,0:T(8,128)(2,1)S(1)} %get-tuple-element.21), channel_id=1, source_target_pairs={{0,512},{4,516},{8,520},{12,524},{512,0},{516,4},{520,8},{524,12},... | collective-permute-start | bytes 147464 | tf_op jit(solution)/shard_map/ppermute | solution.py:260
  25.3 3.5 %collective-permute-start.2 = (bf16[192,128]{1,0:T(8,128)(2,1)S(1)}, bf16[192,128]{1,0:T(8,128)(2,1)S(1)}, u32[]{:S(2)}, u32[]{:S(2)}) collective-permute-start(bf16[192,128]{1,0:T(8,128)(2,1)S(1)} %get-tuple-element.22), channel_id=1, source_target_pairs={{0,520},{4,524},{8,512},{12,516},{512,8},{516,12},{520,0},{524,4},... | collective-permute-start | bytes 147464 | tf_op jit(solution)/shard_map/ppermute | solution.py:260
  28.8 0.0 collective-permute-done.t1
  28.8 0.0 collective-permute-done.1.t2
  28.9 2.1 %collective-permute-done.2.t3 = bf16[192,128]{1,0:T(8,128)(2,1)S(1)} collective-permute-done((bf16[192,128]{1,0:T(8,128)(2,1)S(1)}, bf16[192,128]{1,0:T(8,128)(2,1)S(1)}, u32[]{:S(2)}, u32[]{:S(2)}) %collective-permute-start.2) | collective-permute-done | bytes 49184 | tf_op jit(solution)/shard_map/ppermute | solution.py:260
  31.0 0.0 copy-start.3
  31.0 0.0 all-to-all-done.arrived.h
  31.0 0.0 copy-done.7
  31.0 0.0 copy-done.8
  31.0 1.5 shard_map.70
  32.5 0.0 copy-done.3
  32.5 23.4 %all-to-all-start.1 = ((bf16[8,64,128]{2,1,0:T(8,128)(2,1)}), bf16[8,64,128]{2,1,0:T(8,128)(2,1)S(1)}, u32[]{:S(2)}, u32[]{:S(2)}) async-start(bf16[8,64,128]{2,1,0:T(8,128)(2,1)} %shard_map.70), calls=%async_computation.1 | async-start | bytes 262144 | tf_op jit(solution)/shard_map/all_to_all | solution.py:246
  55.9 0.1 fusion
  56.0 3.6 %collective-permute-start.4 = (bf16[4,400,128]{2,1,0:T(8,128)(2,1)S(1)}, bf16[4,400,128]{2,1,0:T(8,128)(2,1)S(1)}, u32[]{:S(2)}, u32[]{:S(2)}) collective-permute-start(bf16[4,400,128]{2,1,0:T(8,128)(2,1)S(1)} %get-tuple-element.36), channel_id=1, source_target_pairs={{0,516},{4,512},{8,524},{12,520},{512,4},{516,0},{520,12},{524,8},... | collective-permute-start | bytes 1228808 | tf_op jit(solution)/shard_map/ppermute | solution.py:260
  59.5 2.3 %collective-permute-start.3 = (bf16[4,400,128]{2,1,0:T(8,128)(2,1)S(1)}, bf16[4,400,128]{2,1,0:T(8,128)(2,1)S(1)}, u32[]{:S(2)}, u32[]{:S(2)}) collective-permute-start(bf16[4,400,128]{2,1,0:T(8,128)(2,1)S(1)} %get-tuple-element.37), channel_id=1, source_target_pairs={{0,512},{4,516},{8,520},{12,524},{512,0},{516,4},{520,8},{524,12},... | collective-permute-start | bytes 1228808 | tf_op jit(solution)/shard_map/ppermute | solution.py:260
  61.9 6.7 %collective-permute-done.4.h3 = bf16[4,400,128]{2,1,0:T(8,128)(2,1)S(1)} collective-permute-done((bf16[4,400,128]{2,1,0:T(8,128)(2,1)S(1)}, bf16[4,400,128]{2,1,0:T(8,128)(2,1)S(1)}, u32[]{:S(2)}, u32[]{:S(2)}) %collective-permute-start.4) | collective-permute-done | bytes 409632 | tf_op jit(solution)/shard_map/ppermute | solution.py:260
  68.6 2.6 %collective-permute-done.3.h1 = bf16[4,400,128]{2,1,0:T(8,128)(2,1)S(1)} collective-permute-done((bf16[4,400,128]{2,1,0:T(8,128)(2,1)S(1)}, bf16[4,400,128]{2,1,0:T(8,128)(2,1)S(1)}, u32[]{:S(2)}, u32[]{:S(2)}) %collective-permute-start.3) | collective-permute-done | bytes 409632 | tf_op jit(solution)/shard_map/ppermute | solution.py:260
  71.2 0.0 all-to-all-done.1.pieces
  71.2 0.8 shard_map.71
  72.0 3.5 %all-to-all-start.2 = ((bf16[4,512,128]{2,1,0:T(8,128)(2,1)}), bf16[4,512,128]{2,1,0:T(8,128)(2,1)S(1)}, u32[]{:S(2)}, u32[]{:S(2)}) async-start(bf16[4,512,128]{2,1,0:T(8,128)(2,1)} %shard_map.71), calls=%async_computation.2 | async-start | bytes 1048576 | tf_op jit(solution)/shard_map/all_to_all | solution.py:255
  75.5 4.8 %collective-permute-start.5 = (bf16[8,400,128]{2,1,0:T(8,128)(2,1)S(1)}, bf16[8,400,128]{2,1,0:T(8,128)(2,1)S(1)}, u32[]{:S(2)}, u32[]{:S(2)}) collective-permute-start(bf16[8,400,128]{2,1,0:T(8,128)(2,1)S(1)} %all-to-all-done.arrived.h), channel_id=1, source_target_pairs={{0,8},{4,12},{8,0},{12,4},{512,520},{516,524},{520,512},{524,516},... | collective-permute-start | bytes 2457608 | tf_op jit(solution)/shard_map/ppermute | solution.py:260
  80.3 1.9 %collective-permute-start.6 = (bf16[4,400,128]{2,1,0:T(8,128)(2,1)S(1)}, bf16[4,400,128]{2,1,0:T(8,128)(2,1)S(1)}, u32[]{:S(2)}, u32[]{:S(2)}) collective-permute-start(bf16[4,400,128]{2,1,0:T(8,128)(2,1)S(1)} %collective-permute-done.3.h1), channel_id=1, source_target_pairs={{0,8},{4,12},{8,0},{12,4},{512,520},{516,524},{520,512},{524,516},... | collective-permute-start | bytes 1228808 | tf_op jit(solution)/shard_map/ppermute | solution.py:260
  82.3 2.4 %collective-permute-start.7 = (bf16[4,400,128]{2,1,0:T(8,128)(2,1)S(1)}, bf16[4,400,128]{2,1,0:T(8,128)(2,1)S(1)}, u32[]{:S(2)}, u32[]{:S(2)}) collective-permute-start(bf16[4,400,128]{2,1,0:T(8,128)(2,1)S(1)} %collective-permute-done.4.h3), channel_id=1, source_target_pairs={{0,8},{4,12},{8,0},{12,4},{512,520},{516,524},{520,512},{524,516},... | collective-permute-start | bytes 1228808 | tf_op jit(solution)/shard_map/ppermute | solution.py:260
  84.7 0.0 collective-permute-done.5.g
  84.7 0.0 collective-permute-done.6.g1
  84.7 1.3 collective-permute-done.7.g3
  86.0 0.0 copy-start.1
  86.0 0.8 copy-done.1
  86.8 0.0 all-to-all-done.2.weights
  86.8 0.0 copy-start.2
  86.8 1.0 copy-done.2
  87.8 0.0 copy-start.4
  87.8 0.8 copy-done.4
  88.6 1.6 %shard_map.72 = (bf16[192,128]{1,0:T(8,128)(2,1)S(1)}, bf16[192,128]{1,0:T(8,128)(2,1)S(1)}, bf16[192,128]{1,0:T(8,128)(2,1)S(1)}, bf16[192,128]{1,0:T(8,128)(2,1)S(1)}, bf16[4,512,128]{2,1,0:T(8,128)(2,1)S(1)}) custom-call(bf16[8,400,128]{2,1,0:T(8,128)(2,1)S(1)} %all-to-all-done.arrived.h, bf16[4,400,128]{2,1,0:T(8,128)(2,1)S(1)} %collective-permute-done.3.h1, ...), custom_call_target="tpu_custom_call" | custom-call | tf_op jit(solution)/shard_map/pallas_call | solution.py:48
  90.2 0.0 copy-start.11
  90.2 0.6 copy-done.11
  90.9 0.0 copy-start.5
  90.9 0.0 copy-start.9
  90.9 18.9 %all_to_all.30.parts = bf16[4,512,128]{2,1,0:T(8,128)(2,1)S(1)} all-to-all(bf16[4,512,128]{2,1,0:T(8,128)(2,1)S(1)} %get-tuple-element.31), channel_id=1, replica_groups={{0,16,32,48},{72,88,40,56},{64,80,96,112},{136,152,104,120},{128,144,16..., dimensions={0} | all-to-all | bytes 1048576 | tf_op jit(solution)/shard_map/all_to_all | solution.py:255
  109.7 0.0 copy-done.5
  109.8 0.0 copy-done.9
  109.8 0.0 copy-done.10
  109.8 0.7 shard_map.73
  110.5 21.4 %all-to-all-start.4 = ((bf16[8,64,128]{2,1,0:T(8,128)(2,1)}), bf16[8,64,128]{2,1,0:T(8,128)(2,1)S(1)}, u32[]{:S(2)}, u32[]{:S(2)}) async-start(bf16[8,64,128]{2,1,0:T(8,128)(2,1)} %shard_map.73), calls=%async_computation.4 | async-start | bytes 262144 | tf_op jit(solution)/shard_map/all_to_all | solution.py:246
  131.9 0.0 copy-done.12
  131.9 2.2 %collective-permute-start.8 = (bf16[192,128]{1,0:T(8,128)(2,1)S(1)}, bf16[192,128]{1,0:T(8,128)(2,1)S(1)}, u32[]{:S(2)}, u32[]{:S(2)}) collective-permute-start(bf16[192,128]{1,0:T(8,128)(2,1)S(1)} %copy-done.12), channel_id=1, source_target_pairs={{0,8},{4,12},{8,0},{12,4},{512,520},{516,524},{520,512},{524,516},... | collective-permute-start | bytes 147464 | tf_op jit(solution)/shard_map/ppermute | solution.py:260
  134.1 2.3 %collective-permute-start.9 = (bf16[192,128]{1,0:T(8,128)(2,1)}, bf16[192,128]{1,0:T(8,128)(2,1)S(1)}, u32[]{:S(2)}, u32[]{:S(2)}) collective-permute-start(bf16[192,128]{1,0:T(8,128)(2,1)} %copy-done.10), channel_id=1, source_target_pairs={{0,512},{4,516},{8,520},{12,524},{512,0},{516,4},{520,8},{524,12},... | collective-permute-start | bytes 147464 | tf_op jit(solution)/shard_map/ppermute | solution.py:260
  136.4 3.3 %collective-permute-start.10 = (bf16[192,128]{1,0:T(8,128)(2,1)}, bf16[192,128]{1,0:T(8,128)(2,1)S(1)}, u32[]{:S(2)}, u32[]{:S(2)}) collective-permute-start(bf16[192,128]{1,0:T(8,128)(2,1)} %copy-done.9), channel_id=1, source_target_pairs={{0,520},{4,524},{8,512},{12,516},{512,8},{516,12},{520,0},{524,4},... | collective-permute-start | bytes 147464 | tf_op jit(solution)/shard_map/ppermute | solution.py:260
  139.7 0.0 collective-permute-done.8.p1
  139.7 0.0 collective-permute-done.9.p2
  139.8 2.9 %collective-permute-done.10.p3 = bf16[192,128]{1,0:T(8,128)(2,1)S(1)} collective-permute-done((bf16[192,128]{1,0:T(8,128)(2,1)}, bf16[192,128]{1,0:T(8,128)(2,1)S(1)}, u32[]{:S(2)}, u32[]{:S(2)}) %collective-permute-start.10) | collective-permute-done | bytes 49184 | tf_op jit(solution)/shard_map/ppermute | solution.py:260
  142.6 0.8 copy-done.6
  143.4 0.4 shard_map.74.blocks
  143.8 0.1 all-to-all-done.4.parts
  144.0 12.0 %all_to_all.31.refs_0_ = bf16[8,112,128]{2,1,0:T(8,128)(2,1)S(1)} all-to-all(bf16[8,112,128]{2,1,0:T(8,128)(2,1)S(1)} %shard_map.75), channel_id=1, replica_groups=mesh['ylo'=2,'zh'=8,'zl'=4,'core'=2,'yhi'=2,'x'=4] {'yhi','x'}, dimensions={0} | all-to-all | bytes 458752 | tf_op jit(solution)/shard_map/all_to_all | solution.py:246
  155.9 1.2 shard_map.76
  (4 shorter events, 0.0 us)
Async XLA Ops:
  0.6 9.9 %copy-start = (bf16[192,4096]{1,0:T(8,128)(2,1)S(1)}, bf16[192,4096]{1,0:T(8,128)(2,1)}, u32[]{:S(2)}) copy-start(bf16[192,4096]{1,0:T(8,128)(2,1)} %target.1) | copy-start | bytes 4718596
  3.0 28.0 %copy-start.7 = (s32[16]{0:T(128)S(1)}, s32[16]{0:T(128)}, u32[]{:S(2)}) copy-start(s32[16]{0:T(128)} %kept.3) | copy-start | bytes 196
  3.0 28.0 %copy-start.8 = (s32[16]{0:T(128)S(1)}, s32[16]{0:T(128)}, u32[]{:S(2)}) copy-start(s32[16]{0:T(128)} %slot.1) | copy-start | bytes 196
  3.0 28.0 %all-to-all-start = ((bf16[8,400,128]{2,1,0:T(8,128)(2,1)}), bf16[8,400,128]{2,1,0:T(8,128)(2,1)S(1)}, u32[]{:S(2)}, u32[]{:S(2)}) async-start(bf16[8,400,128]{2,1,0:T(8,128)(2,1)} %shard_map.68), calls=%async_computation | async-start | bytes 1638400 | tf_op jit(solution)/shard_map/all_to_all | solution.py:246
  11.2 17.6 %collective-permute-start = (bf16[192,128]{1,0:T(8,128)(2,1)S(1)}, bf16[192,128]{1,0:T(8,128)(2,1)S(1)}, u32[]{:S(2)}, u32[]{:S(2)}) collective-permute-start(bf16[192,128]{1,0:T(8,128)(2,1)S(1)} %get-tuple-element.20), channel_id=1, source_target_pairs={{0,8},{4,12},{8,0},{12,4},{512,520},{516,524},{520,512},{524,516},... | collective-permute-start | bytes 147464 | tf_op jit(solution)/shard_map/ppermute | solution.py:260
  23.4 5.5 %collective-permute-start.1 = (bf16[192,128]{1,0:T(8,128)(2,1)S(1)}, bf16[192,128]{1,0:T(8,128)(2,1)S(1)}, u32[]{:S(2)}, u32[]{:S(2)}) collective-permute-start(bf16[192,128]{1,0:T(8,128)(2,1)S(1)} %get-tuple-element.21), channel_id=1, source_target_pairs={{0,512},{4,516},{8,520},{12,524},{512,0},{516,4},{520,8},{524,12},... | collective-permute-start | bytes 147464 | tf_op jit(solution)/shard_map/ppermute | solution.py:260
  25.3 5.7 %collective-permute-start.2 = (bf16[192,128]{1,0:T(8,128)(2,1)S(1)}, bf16[192,128]{1,0:T(8,128)(2,1)S(1)}, u32[]{:S(2)}, u32[]{:S(2)}) collective-permute-start(bf16[192,128]{1,0:T(8,128)(2,1)S(1)} %get-tuple-element.22), channel_id=1, source_target_pairs={{0,520},{4,524},{8,512},{12,516},{512,8},{516,12},{520,0},{524,4},... | collective-permute-start | bytes 147464 | tf_op jit(solution)/shard_map/ppermute | solution.py:260
  31.0 1.5 copy-start.3
  32.5 38.7 %all-to-all-start.1 = ((bf16[8,64,128]{2,1,0:T(8,128)(2,1)}), bf16[8,64,128]{2,1,0:T(8,128)(2,1)S(1)}, u32[]{:S(2)}, u32[]{:S(2)}) async-start(bf16[8,64,128]{2,1,0:T(8,128)(2,1)} %shard_map.70), calls=%async_computation.1 | async-start | bytes 262144 | tf_op jit(solution)/shard_map/all_to_all | solution.py:246
  56.0 12.6 %collective-permute-start.4 = (bf16[4,400,128]{2,1,0:T(8,128)(2,1)S(1)}, bf16[4,400,128]{2,1,0:T(8,128)(2,1)S(1)}, u32[]{:S(2)}, u32[]{:S(2)}) collective-permute-start(bf16[4,400,128]{2,1,0:T(8,128)(2,1)S(1)} %get-tuple-element.36), channel_id=1, source_target_pairs={{0,516},{4,512},{8,524},{12,520},{512,4},{516,0},{520,12},{524,8},... | collective-permute-start | bytes 1228808 | tf_op jit(solution)/shard_map/ppermute | solution.py:260
  59.5 11.6 %collective-permute-start.3 = (bf16[4,400,128]{2,1,0:T(8,128)(2,1)S(1)}, bf16[4,400,128]{2,1,0:T(8,128)(2,1)S(1)}, u32[]{:S(2)}, u32[]{:S(2)}) collective-permute-start(bf16[4,400,128]{2,1,0:T(8,128)(2,1)S(1)} %get-tuple-element.37), channel_id=1, source_target_pairs={{0,512},{4,516},{8,520},{12,524},{512,0},{516,4},{520,8},{524,12},... | collective-permute-start | bytes 1228808 | tf_op jit(solution)/shard_map/ppermute | solution.py:260
  72.0 14.8 %all-to-all-start.2 = ((bf16[4,512,128]{2,1,0:T(8,128)(2,1)}), bf16[4,512,128]{2,1,0:T(8,128)(2,1)S(1)}, u32[]{:S(2)}, u32[]{:S(2)}) async-start(bf16[4,512,128]{2,1,0:T(8,128)(2,1)} %shard_map.71), calls=%async_computation.2 | async-start | bytes 1048576 | tf_op jit(solution)/shard_map/all_to_all | solution.py:255
  75.5 9.2 %collective-permute-start.5 = (bf16[8,400,128]{2,1,0:T(8,128)(2,1)S(1)}, bf16[8,400,128]{2,1,0:T(8,128)(2,1)S(1)}, u32[]{:S(2)}, u32[]{:S(2)}) collective-permute-start(bf16[8,400,128]{2,1,0:T(8,128)(2,1)S(1)} %all-to-all-done.arrived.h), channel_id=1, source_target_pairs={{0,8},{4,12},{8,0},{12,4},{512,520},{516,524},{520,512},{524,516},... | collective-permute-start | bytes 2457608 | tf_op jit(solution)/shard_map/ppermute | solution.py:260
  80.3 4.4 %collective-permute-start.6 = (bf16[4,400,128]{2,1,0:T(8,128)(2,1)S(1)}, bf16[4,400,128]{2,1,0:T(8,128)(2,1)S(1)}, u32[]{:S(2)}, u32[]{:S(2)}) collective-permute-start(bf16[4,400,128]{2,1,0:T(8,128)(2,1)S(1)} %collective-permute-done.3.h1), channel_id=1, source_target_pairs={{0,8},{4,12},{8,0},{12,4},{512,520},{516,524},{520,512},{524,516},... | collective-permute-start | bytes 1228808 | tf_op jit(solution)/shard_map/ppermute | solution.py:260
  82.3 3.8 %collective-permute-start.7 = (bf16[4,400,128]{2,1,0:T(8,128)(2,1)S(1)}, bf16[4,400,128]{2,1,0:T(8,128)(2,1)S(1)}, u32[]{:S(2)}, u32[]{:S(2)}) collective-permute-start(bf16[4,400,128]{2,1,0:T(8,128)(2,1)S(1)} %collective-permute-done.4.h3), channel_id=1, source_target_pairs={{0,8},{4,12},{8,0},{12,4},{512,520},{516,524},{520,512},{524,516},... | collective-permute-start | bytes 1228808 | tf_op jit(solution)/shard_map/ppermute | solution.py:260
  86.0 0.8 copy-start.1
  86.8 1.0 copy-start.2
  87.8 0.8 copy-start.4
  90.2 0.6 copy-start.11
  90.9 18.9 %copy-start.5 = (bf16[192,128]{1,0:T(8,128)(2,1)}, bf16[192,128]{1,0:T(8,128)(2,1)S(1)}, u32[]{:S(2)}) copy-start(bf16[192,128]{1,0:T(8,128)(2,1)S(1)} %get-tuple-element.32.p0) | copy-start | bytes 147460
  90.9 18.9 %copy-start.9 = (bf16[192,128]{1,0:T(8,128)(2,1)}, bf16[192,128]{1,0:T(8,128)(2,1)S(1)}, u32[]{:S(2)}) copy-start(bf16[192,128]{1,0:T(8,128)(2,1)S(1)} %get-tuple-element.35) | copy-start | bytes 147460
  90.9 18.9 %copy-start.10 = (bf16[192,128]{1,0:T(8,128)(2,1)}, bf16[192,128]{1,0:T(8,128)(2,1)S(1)}, u32[]{:S(2)}) copy-start(bf16[192,128]{1,0:T(8,128)(2,1)S(1)} %get-tuple-element.34) | copy-start | bytes 147460
  90.9 41.0 %copy-start.12 = (bf16[192,128]{1,0:T(8,128)(2,1)S(1)}, bf16[192,128]{1,0:T(8,128)(2,1)}, u32[]{:S(2)}) copy-start(bf16[192,128]{1,0:T(8,128)(2,1)} %copy-done.11) | copy-start | bytes 147460
  110.5 33.4 %all-to-all-start.4 = ((bf16[8,64,128]{2,1,0:T(8,128)(2,1)}), bf16[8,64,128]{2,1,0:T(8,128)(2,1)S(1)}, u32[]{:S(2)}, u32[]{:S(2)}) async-start(bf16[8,64,128]{2,1,0:T(8,128)(2,1)} %shard_map.73), calls=%async_computation.4 | async-start | bytes 262144 | tf_op jit(solution)/shard_map/all_to_all | solution.py:246
  131.9 7.9 %collective-permute-start.8 = (bf16[192,128]{1,0:T(8,128)(2,1)S(1)}, bf16[192,128]{1,0:T(8,128)(2,1)S(1)}, u32[]{:S(2)}, u32[]{:S(2)}) collective-permute-start(bf16[192,128]{1,0:T(8,128)(2,1)S(1)} %copy-done.12), channel_id=1, source_target_pairs={{0,8},{4,12},{8,0},{12,4},{512,520},{516,524},{520,512},{524,516},... | collective-permute-start | bytes 147464 | tf_op jit(solution)/shard_map/ppermute | solution.py:260
  134.1 5.6 %collective-permute-start.9 = (bf16[192,128]{1,0:T(8,128)(2,1)}, bf16[192,128]{1,0:T(8,128)(2,1)S(1)}, u32[]{:S(2)}, u32[]{:S(2)}) collective-permute-start(bf16[192,128]{1,0:T(8,128)(2,1)} %copy-done.10), channel_id=1, source_target_pairs={{0,512},{4,516},{8,520},{12,524},{512,0},{516,4},{520,8},{524,12},... | collective-permute-start | bytes 147464 | tf_op jit(solution)/shard_map/ppermute | solution.py:260
  136.4 6.2 %collective-permute-start.10 = (bf16[192,128]{1,0:T(8,128)(2,1)}, bf16[192,128]{1,0:T(8,128)(2,1)S(1)}, u32[]{:S(2)}, u32[]{:S(2)}) collective-permute-start(bf16[192,128]{1,0:T(8,128)(2,1)} %copy-done.9), channel_id=1, source_target_pairs={{0,520},{4,524},{8,512},{12,516},{512,8},{516,12},{520,0},{524,4},... | collective-permute-start | bytes 147464 | tf_op jit(solution)/shard_map/ppermute | solution.py:260
  142.6 0.8 copy-start.6

commit v5 on v4

--- a/solution.py
+++ b/solution.py
@@ -294,7 +294,7 @@
         compiler_params=PARAMS,
     )(kept, slot, row)
     pieces = exchange(piece, "zh", GATHER)
-    beside = [shift(row[:4], y=1), shift(row[4:], y=3)]
+    beside = [shift(row[:4, : 2 * TOK], y=1), shift(row[4:, : 2 * TOK], y=3)]
     pieces, beside = lax.optimization_barrier((pieces, beside))
     grouped = call(regroup_kernel, shape((NL, 512, 128), BF16), [VMEM], pieces)
     weights = exchange_near(grouped)
@@ -309,12 +309,15 @@
         *others,
         weights,
         *targets,
+        params=WHOLE,
     )
 
     parts = exchange_near(gradient)
+    near = shift(outs[1], core=1)
+    parts, near = lax.optimization_barrier((parts, near))
     summed = call(first_sum_kernel, shape((NH, 64, 128), BF16), [VMEM], parts)
     parts = exchange(summed, "zh", SCATTER)
-    groups = pairs(*outs)
+    groups = [outs[0], near, shift(outs[2], y=1), shift(outs[3], y=1, core=1)]
     blocks = call(
         spread_kernel, shape((NT, 96, 128), BF16), [SMEM] * 2 + [VMEM] * 4, *place[:2], *groups
     )

time: 158 us -> 157 us (level)
  blocking collectives: 30.8 us -> 12.6 us
  waiting for transfers between devices: 15.8 us -> 27.8 us
  starting transfers between devices: 96.3 us -> 101 us
  Pallas kernels: 9.18 us -> 12.1 us
  local copies, waits for them, and re-layouts: 4.05 us -> 1.5 us
    all_to_all x1 -> x0, blocking collectives: 18.9 us -> none  [exchange_near(): lax.all_to_all(x, ('zh', 'zl', 'core'), 0, 0, axis_index_groups=groups)]
    all_to_all x1 -> x2, waiting for transfers between devices: 0.01 us -> 9.32 us  [exchange_near(): lax.all_to_all(x, ('zh', 'zl', 'core'), 0, 0, axis_index_groups=groups)]
    all_to_all x1 -> x2, starting transfers between devices: 3.47 us -> 9.39 us  [exchange_near(): lax.all_to_all(x, ('zh', 'zl', 'core'), 0, 0, axis_index_groups=groups)]
    pallas_call x8, Pallas kernels: 7.69 us -> 10.6 us  [call(): pl.pallas_call(kernel, out_shape=out, in_specs=specs, out_specs=jax.tree....]
    unnamed x26 -> x32, local copies, waits for them, and re-layouts: 4 us -> 1.45 us
  transfers between devices with their start and end apart: 15 -> 16, of which waited for: 6 -> 9; matrix products, arithmetic and copies ran while one was open for 0% -> 0% of each run, Pallas kernels for 1% -> 1%
where the time goes in v5:
time: 157 us; the launch traced here: 156 us
  starting transfers between devices  101 us (64%)
  waiting for transfers between devices  27.8 us (18%)
  blocking collectives  12.6 us (8%)
  Pallas kernels  12.1 us (8%)
    all_to_all x3, starting transfers between devices, exchange(): return lax.all_to_all(x, axes, 0, 0, axis_index_groups=groups)  51.8 us
    ppermute x11, starting transfers between devices, shift(): lax.ppermute(a, ('ylo', 'core', 'yhi'), [(i, i ^ bits) for i in range(8)])  39.9 us
    ppermute x11, waiting for transfers between devices, shift(): lax.ppermute(a, ('ylo', 'core', 'yhi'), [(i, i ^ bits) for i in range(8)])  17.1 us
    all_to_all x1, blocking collectives, exchange(): return lax.all_to_all(x, axes, 0, 0, axis_index_groups=groups)  12.6 us
    pallas_call x8, Pallas kernels, call(): pl.pallas_call(kernel, out_shape=out, in_specs=specs, out_specs=jax.tree....  10.6 us
    all_to_all x2, starting transfers between devices, exchange_near(): lax.all_to_all(x, ('zh', 'zl', 'core'), 0, 0, axis_index_groups=groups)  9.39 us
    all_to_all x2, waiting for transfers between devices, exchange_near(): lax.all_to_all(x, ('zh', 'zl', 'core'), 0, 0, axis_index_groups=groups)  9.32 us
  transfers between devices with their start and end apart: 16, of which 9 were waited for; matrix products, arithmetic and copies ran while one was open for 0% of the time, Pallas kernels for 1%

profile of v5, /device:TPU:1, one launch (start us, length us, event | category | flops | bytes accessed | tf_op | source)
XLA Modules:
  0.0 156.0 jit_solution(6648845339479717590)
XLA Ops:
  0.6 0.0 copy-start.1
  0.6 2.3 %shard_map.68 = bf16[8,400,128]{2,1,0:T(8,128)(2,1)} custom-call(s32[16]{0:T(128)} %kept.3, s32[1]{0:T(128)} %bitcast.me, bf16[32,3584]{1,0:T(8,128)(2,1)} %teacher.1, bf16[192,256]{1,0:T(8,128)(2,1)} %hidden.1), custom_call_target="tpu_custom_call" | custom-call | tf_op jit(solution)/shard_map/pallas_call | solution.py:48
  3.0 7.6 %all-to-all-start = ((bf16[8,400,128]{2,1,0:T(8,128)(2,1)}), bf16[8,400,128]{2,1,0:T(8,128)(2,1)S(1)}, u32[]{:S(2)}, u32[]{:S(2)}) async-start(bf16[8,400,128]{2,1,0:T(8,128)(2,1)} %shard_map.68), calls=%async_computation | async-start | bytes 1638400 | tf_op jit(solution)/shard_map/all_to_all | solution.py:246
  10.6 0.0 copy-done.1
  10.6 0.6 shard_map.69
  11.2 0.0 copy-start.2
  11.2 0.6 copy-done.2
  11.8 12.1 %collective-permute-start = (bf16[192,128]{1,0:T(8,128)(2,1)S(1)}, bf16[192,128]{1,0:T(8,128)(2,1)S(1)}, u32[]{:S(2)}, u32[]{:S(2)}) collective-permute-start(bf16[192,128]{1,0:T(8,128)(2,1)S(1)} %get-tuple-element.22), channel_id=1, source_target_pairs={{0,8},{4,12},{8,0},{12,4},{512,520},{516,524},{520,512},{524,516},... | collective-permute-start | bytes 147464 | tf_op jit(solution)/shard_map/ppermute | solution.py:260
  24.0 1.9 %collective-permute-start.1 = (bf16[192,128]{1,0:T(8,128)(2,1)S(1)}, bf16[192,128]{1,0:T(8,128)(2,1)S(1)}, u32[]{:S(2)}, u32[]{:S(2)}) collective-permute-start(bf16[192,128]{1,0:T(8,128)(2,1)S(1)} %get-tuple-element.23), channel_id=1, source_target_pairs={{0,512},{4,516},{8,520},{12,524},{512,0},{516,4},{520,8},{524,12},... | collective-permute-start | bytes 147464 | tf_op jit(solution)/shard_map/ppermute | solution.py:260
  25.9 3.5 %collective-permute-start.2 = (bf16[192,128]{1,0:T(8,128)(2,1)S(1)}, bf16[192,128]{1,0:T(8,128)(2,1)S(1)}, u32[]{:S(2)}, u32[]{:S(2)}) collective-permute-start(bf16[192,128]{1,0:T(8,128)(2,1)S(1)} %get-tuple-element.24), channel_id=1, source_target_pairs={{0,520},{4,524},{8,512},{12,516},{512,8},{516,12},{520,0},{524,4},... | collective-permute-start | bytes 147464 | tf_op jit(solution)/shard_map/ppermute | solution.py:260
  29.4 0.0 collective-permute-done.t1
  29.4 0.0 copy-start.11
  29.5 0.0 collective-permute-done.1.t2
  29.5 0.0 copy-start.12
  29.5 2.1 %collective-permute-done.2.t3 = bf16[192,128]{1,0:T(8,128)(2,1)S(1)} collective-permute-done((bf16[192,128]{1,0:T(8,128)(2,1)S(1)}, bf16[192,128]{1,0:T(8,128)(2,1)S(1)}, u32[]{:S(2)}, u32[]{:S(2)}) %collective-permute-start.2) | collective-permute-done | bytes 49184 | tf_op jit(solution)/shard_map/ppermute | solution.py:260
  31.6 0.0 all-to-all-done.arrived.h
  31.6 0.0 copy-done.4
  31.6 0.0 copy-done.5
  31.6 1.5 shard_map.70
  33.1 22.8 %all-to-all-start.1 = ((bf16[8,64,128]{2,1,0:T(8,128)(2,1)}), bf16[8,64,128]{2,1,0:T(8,128)(2,1)S(1)}, u32[]{:S(2)}, u32[]{:S(2)}) async-start(bf16[8,64,128]{2,1,0:T(8,128)(2,1)} %shard_map.70), calls=%async_computation.1 | async-start | bytes 262144 | tf_op jit(solution)/shard_map/all_to_all | solution.py:246
  55.9 0.1 fusion
  56.0 3.7 %collective-permute-start.4 = (bf16[4,384,128]{2,1,0:T(8,128)(2,1)S(1)}, bf16[4,384,128]{2,1,0:T(8,128)(2,1)S(1)}, u32[]{:S(2)}, u32[]{:S(2)}) collective-permute-start(bf16[4,384,128]{2,1,0:T(8,128)(2,1)S(1)} %get-tuple-element.40), channel_id=1, source_target_pairs={{0,516},{4,512},{8,524},{12,520},{512,4},{516,0},{520,12},{524,8},... | collective-permute-start | bytes 1179656 | tf_op jit(solution)/shard_map/ppermute | solution.py:260
  59.7 2.3 %collective-permute-start.3 = (bf16[4,384,128]{2,1,0:T(8,128)(2,1)S(1)}, bf16[4,384,128]{2,1,0:T(8,128)(2,1)S(1)}, u32[]{:S(2)}, u32[]{:S(2)}) collective-permute-start(bf16[4,384,128]{2,1,0:T(8,128)(2,1)S(1)} %get-tuple-element.41), channel_id=1, source_target_pairs={{0,512},{4,516},{8,520},{12,524},{512,0},{516,4},{520,8},{524,12},... | collective-permute-start | bytes 1179656 | tf_op jit(solution)/shard_map/ppermute | solution.py:260
  62.0 6.3 %collective-permute-done.4.h3 = bf16[4,384,128]{2,1,0:T(8,128)(2,1)S(1)} collective-permute-done((bf16[4,384,128]{2,1,0:T(8,128)(2,1)S(1)}, bf16[4,384,128]{2,1,0:T(8,128)(2,1)S(1)}, u32[]{:S(2)}, u32[]{:S(2)}) %collective-permute-start.4) | collective-permute-done | bytes 393248 | tf_op jit(solution)/shard_map/ppermute | solution.py:260
  68.2 2.7 %collective-permute-done.3.h1 = bf16[4,384,128]{2,1,0:T(8,128)(2,1)S(1)} collective-permute-done((bf16[4,384,128]{2,1,0:T(8,128)(2,1)S(1)}, bf16[4,384,128]{2,1,0:T(8,128)(2,1)S(1)}, u32[]{:S(2)}, u32[]{:S(2)}) %collective-permute-start.3) | collective-permute-done | bytes 393248 | tf_op jit(solution)/shard_map/ppermute | solution.py:260
  71.0 0.0 all-to-all-done.1.pieces
  71.0 0.9 shard_map.71
  71.9 0.0 copy-done.11
  71.9 0.0 copy-done.12
  71.9 0.0 copy-done.13
  71.9 3.5 %all-to-all-start.2 = ((bf16[4,512,128]{2,1,0:T(8,128)(2,1)}), bf16[4,512,128]{2,1,0:T(8,128)(2,1)S(1)}, u32[]{:S(2)}, u32[]{:S(2)}) async-start(bf16[4,512,128]{2,1,0:T(8,128)(2,1)} %shard_map.71), calls=%async_computation.2 | async-start | bytes 1048576 | tf_op jit(solution)/shard_map/all_to_all | solution.py:255
  75.4 0.0 copy-done
  75.4 5.0 %collective-permute-start.5 = (bf16[8,400,128]{2,1,0:T(8,128)(2,1)S(1)}, bf16[8,400,128]{2,1,0:T(8,128)(2,1)S(1)}, u32[]{:S(2)}, u32[]{:S(2)}) collective-permute-start(bf16[8,400,128]{2,1,0:T(8,128)(2,1)S(1)} %all-to-all-done.arrived.h), channel_id=1, source_target_pairs={{0,8},{4,12},{8,0},{12,4},{512,520},{516,524},{520,512},{524,516},... | collective-permute-start | bytes 2457608 | tf_op jit(solution)/shard_map/ppermute | solution.py:260
  80.3 1.9 %collective-permute-start.6 = (bf16[4,384,128]{2,1,0:T(8,128)(2,1)S(1)}, bf16[4,384,128]{2,1,0:T(8,128)(2,1)S(1)}, u32[]{:S(2)}, u32[]{:S(2)}) collective-permute-start(bf16[4,384,128]{2,1,0:T(8,128)(2,1)S(1)} %collective-permute-done.3.h1), channel_id=1, source_target_pairs={{0,8},{4,12},{8,0},{12,4},{512,520},{516,524},{520,512},{524,516},... | collective-permute-start | bytes 1179656 | tf_op jit(solution)/shard_map/ppermute | solution.py:260
  82.3 2.4 %collective-permute-start.7 = (bf16[4,384,128]{2,1,0:T(8,128)(2,1)S(1)}, bf16[4,384,128]{2,1,0:T(8,128)(2,1)}, u32[]{:S(2)}, u32[]{:S(2)}) collective-permute-start(bf16[4,384,128]{2,1,0:T(8,128)(2,1)S(1)} %collective-permute-done.4.h3), channel_id=1, source_target_pairs={{0,8},{4,12},{8,0},{12,4},{512,520},{516,524},{520,512},{524,516},... | collective-permute-start | bytes 1179656 | tf_op jit(solution)/shard_map/ppermute | solution.py:260
  84.7 0.0 collective-permute-done.5.g
  84.7 0.0 copy-start.7
  84.7 0.0 collective-permute-done.6.g1
  84.7 0.0 copy-start.10
  84.7 1.4 collective-permute-done.7.g3
  86.2 0.0 all-to-all-done.2.weights
  86.2 0.0 copy-done.8
  86.2 0.0 copy-done.9
  86.2 0.0 copy-done.7
  86.2 0.0 copy-done.10
  86.2 0.0 copy-start.6
  86.2 0.8 copy-done.6
  87.0 4.5 %shard_map.72 = (bf16[192,128]{1,0:T(8,128)(2,1)}, bf16[192,128]{1,0:T(8,128)(2,1)}, bf16[192,128]{1,0:T(8,128)(2,1)}, bf16[192,128]{1,0:T(8,128)(2,1)}, bf16[4,512,128]{2,1,0:T(8,128)(2,1)}) custom-call(bf16[8,400,128]{2,1,0:T(8,128)(2,1)} %copy-done, bf16[4,384,128]{2,1,0:T(8,128)(2,1)} %copy-done.9, bf16[4,384,128]{2,1,0:T(8,128)(2,1)} %copy-done.8, ...), custom_call_target="tpu_custom_call" | custom-call | tf_op jit(solution)/shard_map/pallas_call | solution.py:48
  91.5 5.9 %all-to-all-start.3 = ((bf16[4,512,128]{2,1,0:T(8,128)(2,1)}), bf16[4,512,128]{2,1,0:T(8,128)(2,1)S(1)}, u32[]{:S(2)}, u32[]{:S(2)}) async-start(bf16[4,512,128]{2,1,0:T(8,128)(2,1)} %get-tuple-element.33), calls=%async_computation.3 | async-start | bytes 1048576 | tf_op jit(solution)/shard_map/all_to_all | solution.py:255
  97.4 2.8 %collective-permute-start.8 = (bf16[192,128]{1,0:T(8,128)(2,1)}, bf16[192,128]{1,0:T(8,128)(2,1)S(1)}, u32[]{:S(2)}, u32[]{:S(2)}) collective-permute-start(bf16[192,128]{1,0:T(8,128)(2,1)} %get-tuple-element.34), channel_id=1, source_target_pairs={{0,8},{4,12},{8,0},{12,4},{512,520},{516,524},{520,512},{524,516},... | collective-permute-start | bytes 147464 | tf_op jit(solution)/shard_map/ppermute | solution.py:260
  100.2 1.1 collective-permute-done.8.p1
  101.3 9.3 %all-to-all-done.3.parts = bf16[4,512,128]{2,1,0:T(8,128)(2,1)S(1)} async-done(((bf16[4,512,128]{2,1,0:T(8,128)(2,1)}), bf16[4,512,128]{2,1,0:T(8,128)(2,1)S(1)}, u32[]{:S(2)}, u32[]{:S(2)}) %all-to-all-start.3) | async-done | bytes 524320 | tf_op jit(solution)/shard_map/all_to_all | solution.py:255
  110.6 0.7 shard_map.73
  111.3 21.3 %all-to-all-start.4 = ((bf16[8,64,128]{2,1,0:T(8,128)(2,1)}), bf16[8,64,128]{2,1,0:T(8,128)(2,1)S(1)}, u32[]{:S(2)}, u32[]{:S(2)}) async-start(bf16[8,64,128]{2,1,0:T(8,128)(2,1)} %shard_map.73), calls=%async_computation.4 | async-start | bytes 262144 | tf_op jit(solution)/shard_map/all_to_all | solution.py:246
  132.7 0.0 copy-done.15
  132.7 2.3 %collective-permute-start.9 = (bf16[192,128]{1,0:T(8,128)(2,1)S(1)}, bf16[192,128]{1,0:T(8,128)(2,1)S(1)}, u32[]{:S(2)}, u32[]{:S(2)}) collective-permute-start(bf16[192,128]{1,0:T(8,128)(2,1)S(1)} %copy-done.15), channel_id=1, source_target_pairs={{0,512},{4,516},{8,520},{12,524},{512,0},{516,4},{520,8},{524,12},... | collective-permute-start | bytes 147464 | tf_op jit(solution)/shard_map/ppermute | solution.py:260
  135.0 1.9 %collective-permute-start.10 = (bf16[192,128]{1,0:T(8,128)(2,1)S(1)}, bf16[192,128]{1,0:T(8,128)(2,1)S(1)}, u32[]{:S(2)}, u32[]{:S(2)}) collective-permute-start(bf16[192,128]{1,0:T(8,128)(2,1)S(1)} %copy-done.14), channel_id=1, source_target_pairs={{0,520},{4,524},{8,512},{12,516},{512,8},{516,12},{520,0},{524,4},... | collective-permute-start | bytes 147464 | tf_op jit(solution)/shard_map/ppermute | solution.py:260
  136.9 0.9 collective-permute-done.9.p2
  137.8 2.6 %collective-permute-done.10.p3 = bf16[192,128]{1,0:T(8,128)(2,1)S(1)} collective-permute-done((bf16[192,128]{1,0:T(8,128)(2,1)S(1)}, bf16[192,128]{1,0:T(8,128)(2,1)S(1)}, u32[]{:S(2)}, u32[]{:S(2)}) %collective-permute-start.10) | collective-permute-done | bytes 49184 | tf_op jit(solution)/shard_map/ppermute | solution.py:260
  140.4 0.0 copy-done.3
  140.4 0.4 shard_map.74.blocks
  140.8 1.4 all-to-all-done.4.parts
  142.2 12.6 %all_to_all.30.refs_0_ = bf16[8,112,128]{2,1,0:T(8,128)(2,1)S(1)} all-to-all(bf16[8,112,128]{2,1,0:T(8,128)(2,1)S(1)} %shard_map.75), channel_id=1, replica_groups=mesh['ylo'=2,'zh'=8,'zl'=4,'core'=2,'yhi'=2,'x'=4] {'yhi','x'}, dimensions={0} | all-to-all | bytes 458752 | tf_op jit(solution)/shard_map/all_to_all | solution.py:246
  154.8 1.2 shard_map.76
  (11 shorter events, 0.0 us)
Async XLA Ops:
  0.6 9.9 %copy-start.1 = (bf16[192,4096]{1,0:T(8,128)(2,1)S(1)}, bf16[192,4096]{1,0:T(8,128)(2,1)}, u32[]{:S(2)}) copy-start(bf16[192,4096]{1,0:T(8,128)(2,1)} %target.1) | copy-start | bytes 4718596
  3.0 28.6 %copy-start.4 = (s32[16]{0:T(128)S(1)}, s32[16]{0:T(128)}, u32[]{:S(2)}) copy-start(s32[16]{0:T(128)} %kept.3) | copy-start | bytes 196
  3.0 28.6 %copy-start.5 = (s32[16]{0:T(128)S(1)}, s32[16]{0:T(128)}, u32[]{:S(2)}) copy-start(s32[16]{0:T(128)} %slot.1) | copy-start | bytes 196
  3.0 28.6 %all-to-all-start = ((bf16[8,400,128]{2,1,0:T(8,128)(2,1)}), bf16[8,400,128]{2,1,0:T(8,128)(2,1)S(1)}, u32[]{:S(2)}, u32[]{:S(2)}) async-start(bf16[8,400,128]{2,1,0:T(8,128)(2,1)} %shard_map.68), calls=%async_computation | async-start | bytes 1638400 | tf_op jit(solution)/shard_map/all_to_all | solution.py:246
  11.2 0.6 copy-start.2
  11.8 17.6 %collective-permute-start = (bf16[192,128]{1,0:T(8,128)(2,1)S(1)}, bf16[192,128]{1,0:T(8,128)(2,1)S(1)}, u32[]{:S(2)}, u32[]{:S(2)}) collective-permute-start(bf16[192,128]{1,0:T(8,128)(2,1)S(1)} %get-tuple-element.22), channel_id=1, source_target_pairs={{0,8},{4,12},{8,0},{12,4},{512,520},{516,524},{520,512},{524,516},... | collective-permute-start | bytes 147464 | tf_op jit(solution)/shard_map/ppermute | solution.py:260
  24.0 5.5 %collective-permute-start.1 = (bf16[192,128]{1,0:T(8,128)(2,1)S(1)}, bf16[192,128]{1,0:T(8,128)(2,1)S(1)}, u32[]{:S(2)}, u32[]{:S(2)}) collective-permute-start(bf16[192,128]{1,0:T(8,128)(2,1)S(1)} %get-tuple-element.23), channel_id=1, source_target_pairs={{0,512},{4,516},{8,520},{12,524},{512,0},{516,4},{520,8},{524,12},... | collective-permute-start | bytes 147464 | tf_op jit(solution)/shard_map/ppermute | solution.py:260
  25.9 5.7 %collective-permute-start.2 = (bf16[192,128]{1,0:T(8,128)(2,1)S(1)}, bf16[192,128]{1,0:T(8,128)(2,1)S(1)}, u32[]{:S(2)}, u32[]{:S(2)}) collective-permute-start(bf16[192,128]{1,0:T(8,128)(2,1)S(1)} %get-tuple-element.24), channel_id=1, source_target_pairs={{0,520},{4,524},{8,512},{12,516},{512,8},{516,12},{520,0},{524,4},... | collective-permute-start | bytes 147464 | tf_op jit(solution)/shard_map/ppermute | solution.py:260
  29.4 42.4 %copy-start.11 = (bf16[192,128]{1,0:T(8,128)(2,1)}, bf16[192,128]{1,0:T(8,128)(2,1)S(1)}, u32[]{:S(2)}) copy-start(bf16[192,128]{1,0:T(8,128)(2,1)S(1)} %collective-permute-done.t1) | copy-start | bytes 147460
  29.5 42.4 %copy-start.12 = (bf16[192,128]{1,0:T(8,128)(2,1)}, bf16[192,128]{1,0:T(8,128)(2,1)S(1)}, u32[]{:S(2)}) copy-start(bf16[192,128]{1,0:T(8,128)(2,1)S(1)} %collective-permute-done.1.t2) | copy-start | bytes 147460
  31.6 40.3 %copy-start.13 = (bf16[192,128]{1,0:T(8,128)(2,1)}, bf16[192,128]{1,0:T(8,128)(2,1)S(1)}, u32[]{:S(2)}) copy-start(bf16[192,128]{1,0:T(8,128)(2,1)S(1)} %collective-permute-done.2.t3) | copy-start | bytes 147460
  31.6 43.8 %copy-start = (bf16[8,400,128]{2,1,0:T(8,128)(2,1)}, bf16[8,400,128]{2,1,0:T(8,128)(2,1)S(1)}, u32[]{:S(2)}) copy-start(bf16[8,400,128]{2,1,0:T(8,128)(2,1)S(1)} %all-to-all-done.arrived.h) | copy-start | bytes 2457604
  33.1 37.9 %all-to-all-start.1 = ((bf16[8,64,128]{2,1,0:T(8,128)(2,1)}), bf16[8,64,128]{2,1,0:T(8,128)(2,1)S(1)}, u32[]{:S(2)}, u32[]{:S(2)}) async-start(bf16[8,64,128]{2,1,0:T(8,128)(2,1)} %shard_map.70), calls=%async_computation.1 | async-start | bytes 262144 | tf_op jit(solution)/shard_map/all_to_all | solution.py:246
  56.0 12.3 %collective-permute-start.4 = (bf16[4,384,128]{2,1,0:T(8,128)(2,1)S(1)}, bf16[4,384,128]{2,1,0:T(8,128)(2,1)S(1)}, u32[]{:S(2)}, u32[]{:S(2)}) collective-permute-start(bf16[4,384,128]{2,1,0:T(8,128)(2,1)S(1)} %get-tuple-element.40), channel_id=1, source_target_pairs={{0,516},{4,512},{8,524},{12,520},{512,4},{516,0},{520,12},{524,8},... | collective-permute-start | bytes 1179656 | tf_op jit(solution)/shard_map/ppermute | solution.py:260
  59.7 11.3 %collective-permute-start.3 = (bf16[4,384,128]{2,1,0:T(8,128)(2,1)S(1)}, bf16[4,384,128]{2,1,0:T(8,128)(2,1)S(1)}, u32[]{:S(2)}, u32[]{:S(2)}) collective-permute-start(bf16[4,384,128]{2,1,0:T(8,128)(2,1)S(1)} %get-tuple-element.41), channel_id=1, source_target_pairs={{0,512},{4,516},{8,520},{12,524},{512,0},{516,4},{520,8},{524,12},... | collective-permute-start | bytes 1179656 | tf_op jit(solution)/shard_map/ppermute | solution.py:260
  68.2 17.9 %copy-start.8 = (bf16[4,384,128]{2,1,0:T(8,128)(2,1)}, bf16[4,384,128]{2,1,0:T(8,128)(2,1)S(1)}, u32[]{:S(2)}) copy-start(bf16[4,384,128]{2,1,0:T(8,128)(2,1)S(1)} %collective-permute-done.4.h3) | copy-start | bytes 1179652
  71.0 15.2 %copy-start.9 = (bf16[4,384,128]{2,1,0:T(8,128)(2,1)}, bf16[4,384,128]{2,1,0:T(8,128)(2,1)S(1)}, u32[]{:S(2)}) copy-start(bf16[4,384,128]{2,1,0:T(8,128)(2,1)S(1)} %collective-permute-done.3.h1) | copy-start | bytes 1179652
  71.9 14.3 %all-to-all-start.2 = ((bf16[4,512,128]{2,1,0:T(8,128)(2,1)}), bf16[4,512,128]{2,1,0:T(8,128)(2,1)S(1)}, u32[]{:S(2)}, u32[]{:S(2)}) async-start(bf16[4,512,128]{2,1,0:T(8,128)(2,1)} %shard_map.71), calls=%async_computation.2 | async-start | bytes 1048576 | tf_op jit(solution)/shard_map/all_to_all | solution.py:255
  75.4 9.3 %collective-permute-start.5 = (bf16[8,400,128]{2,1,0:T(8,128)(2,1)S(1)}, bf16[8,400,128]{2,1,0:T(8,128)(2,1)S(1)}, u32[]{:S(2)}, u32[]{:S(2)}) collective-permute-start(bf16[8,400,128]{2,1,0:T(8,128)(2,1)S(1)} %all-to-all-done.arrived.h), channel_id=1, source_target_pairs={{0,8},{4,12},{8,0},{12,4},{512,520},{516,524},{520,512},{524,516},... | collective-permute-start | bytes 2457608 | tf_op jit(solution)/shard_map/ppermute | solution.py:260
  80.3 4.4 %collective-permute-start.6 = (bf16[4,384,128]{2,1,0:T(8,128)(2,1)S(1)}, bf16[4,384,128]{2,1,0:T(8,128)(2,1)S(1)}, u32[]{:S(2)}, u32[]{:S(2)}) collective-permute-start(bf16[4,384,128]{2,1,0:T(8,128)(2,1)S(1)} %collective-permute-done.3.h1), channel_id=1, source_target_pairs={{0,8},{4,12},{8,0},{12,4},{512,520},{516,524},{520,512},{524,516},... | collective-permute-start | bytes 1179656 | tf_op jit(solution)/shard_map/ppermute | solution.py:260
  82.3 3.9 %collective-permute-start.7 = (bf16[4,384,128]{2,1,0:T(8,128)(2,1)S(1)}, bf16[4,384,128]{2,1,0:T(8,128)(2,1)}, u32[]{:S(2)}, u32[]{:S(2)}) collective-permute-start(bf16[4,384,128]{2,1,0:T(8,128)(2,1)S(1)} %collective-permute-done.4.h3), channel_id=1, source_target_pairs={{0,8},{4,12},{8,0},{12,4},{512,520},{516,524},{520,512},{524,516},... | collective-permute-start | bytes 1179656 | tf_op jit(solution)/shard_map/ppermute | solution.py:260
  84.7 1.5 copy-start.7
  84.7 1.4 copy-start.10
  86.2 0.8 copy-start.6
  91.5 41.2 %copy-start.15 = (bf16[192,128]{1,0:T(8,128)(2,1)S(1)}, bf16[192,128]{1,0:T(8,128)(2,1)}, u32[]{:S(2)}) copy-start(bf16[192,128]{1,0:T(8,128)(2,1)} %get-tuple-element.38) | copy-start | bytes 147460
  91.5 43.5 %copy-start.14 = (bf16[192,128]{1,0:T(8,128)(2,1)S(1)}, bf16[192,128]{1,0:T(8,128)(2,1)}, u32[]{:S(2)}) copy-start(bf16[192,128]{1,0:T(8,128)(2,1)} %get-tuple-element.39) | copy-start | bytes 147460
  91.5 48.9 %copy-start.3 = (bf16[192,128]{1,0:T(8,128)(2,1)S(1)}, bf16[192,128]{1,0:T(8,128)(2,1)}, u32[]{:S(2)}) copy-start(bf16[192,128]{1,0:T(8,128)(2,1)} %get-tuple-element.36.p0) | copy-start | bytes 147460
  91.5 19.1 %all-to-all-start.3 = ((bf16[4,512,128]{2,1,0:T(8,128)(2,1)}), bf16[4,512,128]{2,1,0:T(8,128)(2,1)S(1)}, u32[]{:S(2)}, u32[]{:S(2)}) async-start(bf16[4,512,128]{2,1,0:T(8,128)(2,1)} %get-tuple-element.33), calls=%async_computation.3 | async-start | bytes 1048576 | tf_op jit(solution)/shard_map/all_to_all | solution.py:255
  97.4 3.8 %collective-permute-start.8 = (bf16[192,128]{1,0:T(8,128)(2,1)}, bf16[192,128]{1,0:T(8,128)(2,1)S(1)}, u32[]{:S(2)}, u32[]{:S(2)}) collective-permute-start(bf16[192,128]{1,0:T(8,128)(2,1)} %get-tuple-element.34), channel_id=1, source_target_pairs={{0,8},{4,12},{8,0},{12,4},{512,520},{516,524},{520,512},{524,516},... | collective-permute-start | bytes 147464 | tf_op jit(solution)/shard_map/ppermute | solution.py:260
  111.3 30.9 %all-to-all-start.4 = ((bf16[8,64,128]{2,1,0:T(8,128)(2,1)}), bf16[8,64,128]{2,1,0:T(8,128)(2,1)S(1)}, u32[]{:S(2)}, u32[]{:S(2)}) async-start(bf16[8,64,128]{2,1,0:T(8,128)(2,1)} %shard_map.73), calls=%async_computation.4 | async-start | bytes 262144 | tf_op jit(solution)/shard_map/all_to_all | solution.py:246
  132.7 5.1 %collective-permute-start.9 = (bf16[192,128]{1,0:T(8,128)(2,1)S(1)}, bf16[192,128]{1,0:T(8,128)(2,1)S(1)}, u32[]{:S(2)}, u32[]{:S(2)}) collective-permute-start(bf16[192,128]{1,0:T(8,128)(2,1)S(1)} %copy-done.15), channel_id=1, source_target_pairs={{0,512},{4,516},{8,520},{12,524},{512,0},{516,4},{520,8},{524,12},... | collective-permute-start | bytes 147464 | tf_op jit(solution)/shard_map/ppermute | solution.py:260
  135.0 5.4 %collective-permute-start.10 = (bf16[192,128]{1,0:T(8,128)(2,1)S(1)}, bf16[192,128]{1,0:T(8,128)(2,1)S(1)}, u32[]{:S(2)}, u32[]{:S(2)}) collective-permute-start(bf16[192,128]{1,0:T(8,128)(2,1)S(1)} %copy-done.14), channel_id=1, source_target_pairs={{0,520},{4,524},{8,512},{12,516},{512,8},{516,12},{520,0},{524,4},... | collective-permute-start | bytes 147464 | tf_op jit(solution)/shard_map/ppermute | solution.py:260
